TPU v7x, 32 devices: a whole 2x2x4 slice. The times are simulated.
32 devices in a mesh: dp: 16 (over z, x, core), tensor: 2 (over y).
Axes of the slice: x: 2, y: 2, z: 4, core: 2. Of those that a mesh axis runs over, the one named last changes fastest.
Arguments:
- tokens: bfloat16 [32768, 312], P('dp'), may hold values from -6 to 6
- projection: bfloat16 [3, 312, 312], P(None, None, 'tensor'), may hold values from -0.3125 to 0.3125
- offsets: bfloat16 [2, 312], P(None, 'tensor'), may hold values from -3 to 3
- combiner: bfloat16 [312, 312], P('tensor'), may hold values from -3 to 3
- expansion: bfloat16 [312, 1200], P(None, 'tensor'), may hold values from -0.3125 to 0.3125
- thresholds: bfloat16 [1200], P('tensor'), may hold values from -3 to 3
- contraction: bfloat16 [1200, 312], P('tensor'), may hold values from -0.25 to 0.25
- corrections: bfloat16 [2, 312], replicated, may hold values from -3 to 3
- gains: bfloat16 [2, 312], replicated, may hold values from 0.5 to 1.5
- shifts: bfloat16 [2, 312], replicated, may hold values from -3 to 3
- table_rows: int32 [32768], P('dp'), may hold values from 0 to 168, as said below
- table_columns: int32 [32768], P('dp'), may hold values from 0 to 60, as said below
- table_lengths: int32 [32], P('dp'), may hold values from 256 to 1024
- cotangent: bfloat16 [32768, 312], P('dp'), may hold values from -6 to 6
Outputs:
- layer_output: bfloat16 [32768, 312], P('dp')
- input_gradient: float32 [32768, 312], P('dp')
- projection_gradient: float32 [3, 312, 312], P(None, None, 'tensor')
- offsets_gradient: float32 [2, 312], P(None, 'tensor')
- combiner_gradient: float32 [312, 312], P('tensor')
- expansion_gradient: float32 [312, 1200], P(None, 'tensor')
- thresholds_gradient: float32 [1200], P('tensor')
- contraction_gradient: float32 [1200, 312], P('tensor')
- corrections_gradient: float32 [2, 312], replicated
- gains_gradient: float32 [2, 312], replicated
- shifts_gradient: float32 [2, 312], replicated
Inputs may be any that keep to these rules, and one draw needn't show every extreme that they name: `table_rows`: in every table slots 0 to 15 have row 0 and column 0; a table's cells have rows from 1 and columns from 1 upward. `table_columns`: one table is laid out with 60 columns; others with 3 to 60.
All inputs are finite; a program needn't handle non-finite values.
Results may differ from a plain program's by a relative error of at most 0.02.
Values may be sent and summed in bfloat16 or wider, within the bound.
A program may use at most 128 MiB of HBM per device.

v0:
```python
import jax
import jax.numpy as jnp
from jax import lax
from jax.sharding import PartitionSpec as P

HEAD_DIM = 26
L = 1024
BLOCK = 512


EPS = 1e-05
MASKED = -1e30


def layer_norm(resid, gain, shift):
    center = resid - jnp.mean(resid, -1, keepdims=True)
    spread = jnp.mean(center * center, -1, keepdims=True)
    return center * lax.rsqrt(spread + EPS) * gain + shift


def exact_gelu(value):
    return jax.nn.gelu(value, approximate=False)


def visible(rows_query, rows_key, columns_query, columns_key, length):
    live = jnp.arange(rows_key.shape[0]) < length
    seen = (rows_query[:, None] == rows_key[None, :]) | (
        columns_query[:, None] == columns_key[None, :]
    )
    seen = seen | (rows_key[None, :] == 0) | (rows_query[:, None] == 0)
    return seen & live[None, :]


def block_scores(query_block, keys, seen):
    scores = jnp.einsum(
        "qhe,khe->hqk", query_block, keys, preferred_element_type=jnp.float32
    ) * HEAD_DIM ** (-0.5)
    return jnp.where(seen[None], scores, MASKED)


def attend_forward(pieces):
    query, keys, values, rows, columns, length = pieces
    outputs = []
    totals = []
    for start in range(0, L, BLOCK):
        seen = visible(
            rows[start : start + BLOCK], rows, columns[start : start + BLOCK], columns, length
        )
        scores = block_scores(query[start : start + BLOCK], keys, seen)
        peak = jnp.max(scores, -1, keepdims=True)
        expo = jnp.exp(scores - peak)
        summed = jnp.sum(expo, -1, keepdims=True)
        weights = (expo / summed).astype(jnp.bfloat16)
        outputs.append(
            jnp.einsum("hqk,khe->qhe", weights, values, preferred_element_type=jnp.float32)
        )
        totals.append(peak[..., 0] + jnp.log(summed[..., 0]))
    return (jnp.concatenate(outputs, 0).astype(jnp.bfloat16), jnp.concatenate(totals, 1))


def attend_backward(pieces):
    query, keys, values, d_context, rows, columns, length, totals = pieces
    scale = HEAD_DIM ** (-0.5)
    d_keys = jnp.zeros(keys.shape, jnp.float32)
    d_values = jnp.zeros(values.shape, jnp.float32)
    d_query = []
    for start in range(0, L, BLOCK):
        query_block = query[start : start + BLOCK]
        grad_block = d_context[start : start + BLOCK]
        seen = visible(
            rows[start : start + BLOCK], rows, columns[start : start + BLOCK], columns, length
        )
        scores = block_scores(query_block, keys, seen)
        probs = jnp.exp(scores - totals[:, start : start + BLOCK, None])
        d_probs = jnp.einsum("qhe,khe->hqk", grad_block, values, preferred_element_type=jnp.float32)
        delta = jnp.sum(probs * d_probs, -1, keepdims=True)
        d_scores = (probs * (d_probs - delta)).astype(jnp.bfloat16)
        d_query.append(
            jnp.einsum("hqk,khe->qhe", d_scores, keys, preferred_element_type=jnp.float32) * scale
        )
        d_keys = (
            d_keys
            + jnp.einsum("hqk,qhe->khe", d_scores, query_block, preferred_element_type=jnp.float32)
            * scale
        )
        d_values = d_values + jnp.einsum(
            "hqk,qhe->khe",
            probs.astype(jnp.bfloat16),
            grad_block,
            preferred_element_type=jnp.float32,
        )
    return (jnp.concatenate(d_query, 0), d_keys, d_values)


def forward_pass(
    tokens,
    projection,
    offsets,
    combiner,
    expansion,
    thresholds,
    contraction,
    corrections,
    gains,
    shifts,
    table_rows,
    table_columns,
    table_lengths,
):
    tables = table_lengths.shape[0]
    heads = projection.shape[2] // HEAD_DIM
    projected = jnp.einsum("td,cde->cte", tokens, projection, preferred_element_type=jnp.float32)
    query = (projected[0] + offsets[0].astype(jnp.float32)).astype(jnp.bfloat16)
    keys = projected[1].astype(jnp.bfloat16)
    values = (projected[2] + offsets[1].astype(jnp.float32)).astype(jnp.bfloat16)
    shaped = (tables, L, heads, HEAD_DIM)
    context, totals = lax.map(
        attend_forward,
        (
            query.reshape(shaped),
            keys.reshape(shaped),
            values.reshape(shaped),
            table_rows.reshape(tables, L),
            table_columns.reshape(tables, L),
            table_lengths,
        ),
    )
    context = context.reshape(tokens.shape[0], heads * HEAD_DIM)
    partial_out = jnp.dot(context, combiner, preferred_element_type=jnp.float32)
    attended = lax.psum(partial_out.astype(jnp.bfloat16), "tensor").astype(jnp.float32)
    resid_one = tokens.astype(jnp.float32) + attended + corrections[0].astype(jnp.float32)
    first = layer_norm(resid_one, gains[0].astype(jnp.float32), shifts[0].astype(jnp.float32))
    first_low = first.astype(jnp.bfloat16)
    pre = jnp.dot(first_low, expansion, preferred_element_type=jnp.float32) + thresholds.astype(
        jnp.float32
    )
    act = exact_gelu(pre).astype(jnp.bfloat16)
    partial_down = jnp.dot(act, contraction, preferred_element_type=jnp.float32)
    down = lax.psum(partial_down.astype(jnp.bfloat16), "tensor").astype(jnp.float32)
    resid_two = first + down + corrections[1].astype(jnp.float32)
    return (query, keys, values, context, totals, resid_one, first_low, pre, act, resid_two)


def shards(
    tokens,
    projection,
    offsets,
    combiner,
    expansion,
    thresholds,
    contraction,
    corrections,
    gains,
    shifts,
    table_rows,
    table_columns,
    table_lengths,
    cotangent,
):
    tables = table_lengths.shape[0]
    heads = projection.shape[2] // HEAD_DIM
    shaped = (tables, L, heads, HEAD_DIM)
    saved = forward_pass(
        tokens,
        projection,
        offsets,
        combiner,
        expansion,
        thresholds,
        contraction,
        corrections,
        gains,
        shifts,
        table_rows,
        table_columns,
        table_lengths,
    )
    gain_two = gains[1].astype(jnp.float32)
    shift_two = shifts[1].astype(jnp.float32)
    layer_output = layer_norm(saved[9], gain_two, shift_two).astype(jnp.bfloat16)
    again = lax.optimization_barrier(
        (tokens, projection, offsets, combiner, expansion, thresholds, contraction, corrections)
    )
    saved = forward_pass(
        again[0],
        again[1],
        again[2],
        again[3],
        again[4],
        again[5],
        again[6],
        again[7],
        gains,
        shifts,
        table_rows,
        table_columns,
        table_lengths,
    )
    query, keys, values, context, totals, resid_one, first_low, pre, act, resid_two = saved
    unused, back_two = jax.vjp(layer_norm, resid_two, gain_two, shift_two)
    d_resid_two, d_gain_two, d_shift_two = back_two(cotangent.astype(jnp.float32))
    d_down_bias = jnp.sum(d_resid_two, 0)
    d_down = d_resid_two.astype(jnp.bfloat16)
    d_contraction = jnp.dot(act.T, d_down, preferred_element_type=jnp.float32)
    d_act = jnp.dot(d_down, contraction.T, preferred_element_type=jnp.float32)
    unused, back_gelu = jax.vjp(exact_gelu, pre)
    d_pre = back_gelu(d_act)[0].astype(jnp.bfloat16)
    d_thresholds = jnp.sum(d_pre.astype(jnp.float32), 0)
    d_expansion = jnp.dot(first_low.T, d_pre, preferred_element_type=jnp.float32)
    feed_part = jnp.dot(d_pre, expansion.T, preferred_element_type=jnp.float32)
    d_first = d_resid_two + lax.psum(feed_part.astype(jnp.bfloat16), "tensor").astype(jnp.float32)
    gain_one = gains[0].astype(jnp.float32)
    shift_one = shifts[0].astype(jnp.float32)
    unused, back_one = jax.vjp(layer_norm, resid_one, gain_one, shift_one)
    d_resid_one, d_gain_one, d_shift_one = back_one(d_first)
    d_out_bias = jnp.sum(d_resid_one, 0)
    d_attended = d_resid_one.astype(jnp.bfloat16)
    d_combiner = jnp.dot(context.T, d_attended, preferred_element_type=jnp.float32)
    d_context = jnp.dot(d_attended, combiner.T, preferred_element_type=jnp.float32).astype(
        jnp.bfloat16
    )
    d_query, d_keys, d_values = lax.map(
        attend_backward,
        (
            query.reshape(shaped),
            keys.reshape(shaped),
            values.reshape(shaped),
            d_context.reshape(shaped),
            table_rows.reshape(tables, L),
            table_columns.reshape(tables, L),
            table_lengths,
            totals,
        ),
    )
    d_stacked = (
        jnp.stack((d_query, d_keys, d_values))
        .reshape(3, tokens.shape[0], heads * HEAD_DIM)
        .astype(jnp.bfloat16)
    )
    summed_stack = jnp.sum(d_stacked.astype(jnp.float32), 1)
    d_offsets = jnp.stack((summed_stack[0], summed_stack[2]))
    d_projection = jnp.einsum("td,cte->cde", tokens, d_stacked, preferred_element_type=jnp.float32)
    input_part = jnp.einsum(
        "cte,cde->td", d_stacked, projection, preferred_element_type=jnp.float32
    )
    input_gradient = d_resid_one + lax.psum(input_part.astype(jnp.bfloat16), "tensor").astype(
        jnp.float32
    )
    d_corrections = jnp.stack((d_out_bias, d_down_bias))
    d_gains = jnp.stack((d_gain_one, d_gain_two))
    d_shifts = jnp.stack((d_shift_one, d_shift_two))
    (
        d_projection,
        d_offsets,
        d_combiner,
        d_expansion,
        d_thresholds,
        d_contraction,
        d_corrections,
        d_gains,
        d_shifts,
    ) = lax.psum(
        (
            d_projection,
            d_offsets,
            d_combiner,
            d_expansion,
            d_thresholds,
            d_contraction,
            d_corrections,
            d_gains,
            d_shifts,
        ),
        "dp",
    )
    return (
        layer_output,
        input_gradient,
        d_projection,
        d_offsets,
        d_combiner,
        d_expansion,
        d_thresholds,
        d_contraction,
        d_corrections,
        d_gains,
        d_shifts,
    )


def solution(mesh):
    return jax.shard_map(
        shards,
        mesh=mesh,
        in_specs=(
            P("dp", None),
            P(None, None, "tensor"),
            P(None, "tensor"),
            P("tensor", None),
            P(None, "tensor"),
            P("tensor"),
            P("tensor", None),
            P(),
            P(),
            P(),
            P("dp"),
            P("dp"),
            P("dp"),
            P("dp", None),
        ),
        out_specs=(
            P("dp", None),
            P("dp", None),
            P(None, None, "tensor"),
            P(None, "tensor"),
            P("tensor", None),
            P(None, "tensor"),
            P("tensor"),
            P("tensor", None),
            P(),
            P(),
            P(),
        ),
        check_vma=False,
    )
```

profile of v0, /device:TPU:0, one launch (start us, length us, event | category | flops | bytes accessed | tf_op | source)
XLA Modules:
  0.0 733.3 jit_solution(451686080953609265)
XLA Ops:
  23.8 52.4 %while.37 = (s32[]{:T(128)}, bf16[2,1024,6,26]{1,3,2,0:T(8,128)(2,1)S(1)}, f32[2,6,1024]{2,1,0:T(8,128)S(1)}, bf16[2,1024,6,26]{1,3,2,0:T(8,128)(2,1)}, s32[2,10...) while((s32[]{:T(128)}, ...), condition=%wide.region_17.18_spmd, body=%wide.region_12.17_spmd.sunk | while | flops 736902144 | bytes 83088040 | solution.py:117
  30.3 3.6 fusion.287
  33.9 4.5 fusion.288
  41.9 3.6 fusion.290
  45.5 4.5 fusion.291
  52.9 3.5 fusion.286
  56.4 3.6 fusion.287
  60.0 4.5 fusion.288
  68.0 3.6 fusion.290
  71.6 4.5 fusion.291
  86.1 3.5 fusion.208
  89.5 3.6 squeeze.74
  103.7 24.3 %all-reduce.10.cloned.1.call-done = bf16[2048,312]{0,1:T(8,128)(2,1)} async-done(((bf16[2048,312]{0,1:T(8,128)(2,1)}), bf16[2048,312]{0,1:T(8,128)(2,1)}) %all-reduce.10.cloned.1.call-update) | async-done | bytes 1277968 | tf_op jit(solution)/shard_map/psum | solution.py:130
  132.7 14.5 %multiply_convert_fusion.2 = (bf16[2048,600]{0,1:T(8,128)(2,1)S(1)}, f32[2048,600]{0,1:T(8,128)}, f32[2048,600]{0,1:T(8,128)}) fusion(f32[600]{0:T(1024)S(1)} %convert_element_type.198, bf16[312,600]{1,0:T(8,128)(2,1)S(1)} %copy-done, f32[2048]{0:T(1024)S(1)} %fusion.160, f32[312]{0:T(512)S(1)} %get-tuple-element.402, f32[312]{0:T(512)S(1)} %get-tuple-element.255, ...), kind=kOutput, calls=%fused_computation.183 | convolution fusion | flops 853622784 | bytes 15240832 | tf_op jit(solution)/shard_map/dot_general | solution.py:134
  151.9 126.9 %while.36 = (s32[]{:T(128)}, bf16[2,1024,6,26]{1,3,2,0:T(8,128)(2,1)}, bf16[2,1024,6,26]{1,3,2,0:T(8,128)(2,1)S(1)}, s32[2,1024]{1,0:T(2,128)S(1)}, s32[2,1024]{...) while((s32[]{:T(128)}, ...), condition=%wide.region_5.6_spmd, body=%wide.region_0.5_spmd.sunk | while | flops 711738368 | bytes 105878176 | solution.py:117
  154.9 6.4 fusion.278
  161.3 16.6 %fusion.279 = (f32[6,512]{1,0:T(8,128)S(1)}, f32[6,512,1024]{2,1,0:T(8,128)}) fusion(f32[6,512,1024]{2,1,0:T(8,128)} %fusion.278, pred[512,1024]{1,0:T(8,128)(4,1)S(1)} %get-tuple-element.604), kind=kOutput, calls=%fused_computation.343.clone.1 | output fusion | flops 18875392 | bytes 25702400 | tf_op jit(solution)/shard_map/while/body/eval_jaxpr/sub | solution.py:51
  177.9 7.2 fusion.280
  185.1 6.4 fusion.281
  191.5 16.6 %fusion.282 = (f32[6,512]{1,0:T(8,128)S(1)}, f32[6,512,1024]{2,1,0:T(8,128)}) fusion(f32[6,512,1024]{2,1,0:T(8,128)} %fusion.281, pred[512,1024]{1,0:T(8,128)(4,1)S(1)} %get-tuple-element.607), kind=kOutput, calls=%fused_computation.344.clone.1 | output fusion | flops 18875392 | bytes 25702400 | tf_op jit(solution)/shard_map/while/body/eval_jaxpr/sub | solution.py:51
  208.1 6.6 fusion.283
  218.4 6.4 fusion.278
  224.7 16.6 %fusion.279 = (f32[6,512]{1,0:T(8,128)S(1)}, f32[6,512,1024]{2,1,0:T(8,128)}) fusion(f32[6,512,1024]{2,1,0:T(8,128)} %fusion.278, pred[512,1024]{1,0:T(8,128)(4,1)S(1)} %get-tuple-element.604), kind=kOutput, calls=%fused_computation.343.clone.1 | output fusion | flops 18875392 | bytes 25702400 | tf_op jit(solution)/shard_map/while/body/eval_jaxpr/sub | solution.py:51
  241.4 6.6 fusion.280
  248.0 6.4 fusion.281
  254.4 16.6 %fusion.282 = (f32[6,512]{1,0:T(8,128)S(1)}, f32[6,512,1024]{2,1,0:T(8,128)}) fusion(f32[6,512,1024]{2,1,0:T(8,128)} %fusion.281, pred[512,1024]{1,0:T(8,128)(4,1)S(1)} %get-tuple-element.607), kind=kOutput, calls=%fused_computation.344.clone.1 | output fusion | flops 18875392 | bytes 25702400 | tf_op jit(solution)/shard_map/while/body/eval_jaxpr/sub | solution.py:51
  271.0 6.6 fusion.283
  288.8 4.2 convert_reduce_fusion
  297.9 72.0 %all-reduce.18.cloned.1.call-done = (bf16[2048,312]{0,1:T(8,128)(2,1)}, bf16[2048,312]{0,1:T(8,128)(2,1)}) async-done(((bf16[2048,312]{0,1:T(8,128)(2,1)}, bf16[2048,312]{0,1:T(8,128)(2,1)}), (bf16[2048,312]{0,1:T(8,128)(2,1)}, bf16[2048,312]{0,1:T(8,128)(2,1)})) %all-reduce.18.cloned.1.call-update) | async-done | bytes 2555920 | tf_op jit(solution)/shard_map/psum | solution.py:130
  381.8 127.8 %while.38 = (s32[]{:T(128)}, bf16[2,1024,6,26]{1,3,2,0:T(8,128)(2,1)}, bf16[2,1024,6,26]{1,3,2,0:T(8,128)(2,1)}, bf16[2,1024,6,26]{1,3,2,0:T(8,128)(2,1)}, bf16[...) while((s32[]{:T(128)}, ...), condition=%wide.region_32.33_spmd, body=%wide.region_29.32_spmd.sunk | while | flops 1737876480 | bytes 236152784 | solution.py:222
  394.1 4.2 fusion.312
  398.3 8.6 %multiply_reduce_fusion.10 = (f32[6,512]{1,0:T(8,128)S(1)}, f32[6,512,1024]{2,1,0:T(8,128)}) fusion(f32[6,512,1024]{2,1,0:T(8,128)S(1)} %fusion.303, f32[6,512]{1,0:T(8,128)S(1)} %get-tuple-element.643, pred[512,1024]{1,0:T(8,128)(4,1)} %copy-done.6, bf16[2,1024,6,26]{1,3,2,0:T(8,128)(2,1)} %get-tuple-element.767, s32[]{:T(128)S(6)} %copy.82, ...), kind=kOutput, calls=%fused_computation.105.clone.1 | convolution fusion | flops 179303424 | bytes 26306048 | tf_op jit(solution)/shard_map/while/body/eval_jaxpr/qhe,khe->hqk/dot_general | solution.py:75
  406.9 9.9 %multiply_convert_fusion.5 = bf16[6,512,1024]{2,1,0:T(8,128)(2,1)} fusion(f32[6,512,1024]{2,1,0:T(8,128)} %get-tuple-element.651, f32[6,512,1024]{2,1,0:T(8,128)S(1)} %fusion.303, f32[6,512]{1,0:T(8,128)S(1)} %get-tuple-element.652, f32[6,512]{1,0:T(8,128)S(1)} %get-tuple-element.643, pred[512,1024]{1,0:T(8,128)(4,1)} %copy-done.6), kind=kLoop, calls=%fused_computation.104.clone.1 | loop fusion | flops 18874368 | bytes 32006144 | tf_op jit(solution)/shard_map/while/body/eval_jaxpr/convert_element_type | solution.py:77
  416.8 4.8 fusion.305
  421.6 8.6 %multiply_reduce_fusion.11 = (f32[6,512]{1,0:T(8,128)S(1)}, f32[6,512,1024]{2,1,0:T(8,128)}) fusion(f32[6,512,1024]{2,1,0:T(8,128)S(1)} %fusion.306, f32[6,512]{1,0:T(8,128)S(1)} %get-tuple-element.653, pred[512,1024]{1,0:T(8,128)(4,1)S(1)} %get-tuple-element.654, bf16[2,1024,6,26]{1,3,2,0:T(8,128)(2,1)} %get-tuple-element.767, s32[]{:T(128)S(6)} %copy.82, ...), kind=kOutput, calls=%fused_computation.108.clone.1 | convolution fusion | flops 179303424 | bytes 26305536 | tf_op jit(solution)/shard_map/while/body/eval_jaxpr/qhe,khe->hqk/dot_general | solution.py:75
  430.1 6.9 multiply_convert_fusion.6
  457.7 4.2 fusion.312
  461.9 8.6 %multiply_reduce_fusion.10 = (f32[6,512]{1,0:T(8,128)S(1)}, f32[6,512,1024]{2,1,0:T(8,128)}) fusion(f32[6,512,1024]{2,1,0:T(8,128)S(1)} %fusion.303, f32[6,512]{1,0:T(8,128)S(1)} %get-tuple-element.643, pred[512,1024]{1,0:T(8,128)(4,1)} %copy-done.6, bf16[2,1024,6,26]{1,3,2,0:T(8,128)(2,1)} %get-tuple-element.767, s32[]{:T(128)S(6)} %copy.82, ...), kind=kOutput, calls=%fused_computation.105.clone.1 | convolution fusion | flops 179303424 | bytes 26306048 | tf_op jit(solution)/shard_map/while/body/eval_jaxpr/qhe,khe->hqk/dot_general | solution.py:75
  470.5 9.9 %multiply_convert_fusion.5 = bf16[6,512,1024]{2,1,0:T(8,128)(2,1)} fusion(f32[6,512,1024]{2,1,0:T(8,128)} %get-tuple-element.651, f32[6,512,1024]{2,1,0:T(8,128)S(1)} %fusion.303, f32[6,512]{1,0:T(8,128)S(1)} %get-tuple-element.652, f32[6,512]{1,0:T(8,128)S(1)} %get-tuple-element.643, pred[512,1024]{1,0:T(8,128)(4,1)} %copy-done.6), kind=kLoop, calls=%fused_computation.104.clone.1 | loop fusion | flops 18874368 | bytes 32006144 | tf_op jit(solution)/shard_map/while/body/eval_jaxpr/convert_element_type | solution.py:77
  480.4 4.8 fusion.305
  485.1 8.6 %multiply_reduce_fusion.11 = (f32[6,512]{1,0:T(8,128)S(1)}, f32[6,512,1024]{2,1,0:T(8,128)}) fusion(f32[6,512,1024]{2,1,0:T(8,128)S(1)} %fusion.306, f32[6,512]{1,0:T(8,128)S(1)} %get-tuple-element.653, pred[512,1024]{1,0:T(8,128)(4,1)S(1)} %get-tuple-element.654, bf16[2,1024,6,26]{1,3,2,0:T(8,128)(2,1)} %get-tuple-element.767, s32[]{:T(128)S(6)} %copy.82, ...), kind=kOutput, calls=%fused_computation.108.clone.1 | convolution fusion | flops 179303424 | bytes 26305536 | tf_op jit(solution)/shard_map/while/body/eval_jaxpr/qhe,khe->hqk/dot_general | solution.py:75
  493.7 6.9 multiply_convert_fusion.6
  524.6 15.3 %convolution_convert_fusion.4 = bf16[2048,312]{0,1:T(8,128)(2,1)} fusion(bf16[600,312]{0,1:T(8,128)(2,1)} %param.26, bf16[312,600]{1,0:T(8,128)(2,1)S(1)} %copy-done, f32[600]{0:T(1024)S(1)} %copy-done.83, bf16[2048,312]{0,1:T(8,128)(2,1)S(1)} %copy-done.14, bf16[2048,312]{0,1:T(8,128)(2,1)S(1)} %copy-done.5, f32[312]{0:T(512)S(1)} %copy-done.65, ...), kind=kOutput, calls=%fused_computation.228 | convolution fusion | flops 1621032960 | bytes 4605184 | tf_op jit(solution)/shard_map/dot_general | solution.py:138
  540.0 4.7 fusion.158
  551.6 61.5 %all-reduce.16.cloned.1.call-done = (bf16[2048,312]{0,1:T(8,128)(2,1)}, bf16[2048,312]{0,1:T(8,128)(2,1)}) async-done(((bf16[2048,312]{0,1:T(8,128)(2,1)}, bf16[2048,312]{0,1:T(8,128)(2,1)}), (bf16[2048,312]{0,1:T(8,128)(2,1)}, bf16[2048,312]{0,1:T(8,128)(2,1)})) %all-reduce.16.cloned.1.call-update) | async-done | bytes 2555920 | tf_op jit(solution)/shard_map/psum | solution.py:139
  613.2 4.0 add_reduce_fusion
  620.0 61.9 %all-reduce = (f32[2,156]{1,0:T(2,128)}, f32[600]{0:T(1024)}, f32[2,312]{1,0:T(2,128)}, f32[2,312]{1,0:T(2,128)}, f32[2,312]{1,0:T(2,128)}) all-reduce(f32[2,156]{1,0:T(2,128)S(1)} %pad_maximum_fusion.3, f32[600]{0:T(1024)S(1)} %copy-done.84, f32[2,312]{1,0:T(2,128)S(1)} %pad_maximum_fusion, ...), channel_id=1, replica_groups=mesh['dp'=16,'tensor'=2] {'dp'}, use_global_device_ids=true, to_apply=%region_36.37 | all-reduce | flops 2784 | bytes 22272 | tf_op jit(solution)/shard_map/psum | solution.py:262
  687.2 31.6 %all-reduce.14.cloned.1.call-done = (f32[3,312,156]{1,2,0:T(8,128)}, f32[156,312]{1,0:T(8,128)}, f32[312,600]{1,0:T(8,128)}, f32[600,312]{0,1:T(8,128)}) async-done(((f32[3,312,156]{1,2,0:T(8,128)}, f32[156,312]{1,0:T(8,128)}, f32[312,600]{1,0:T(8,128)}, f32[600,312]{0,1:T(8,128)}), (f32[3,312,156]{1,2,0:T(8,128)}, f32[156,312]{1,0:T(8,128)}, f32[312,600]{1,0:T(8,128)}, ...) | async-done | bytes 2276368 | tf_op jit(solution)/shard_map/psum | solution.py:262
  (413 shorter events, 174.2 us)
Async XLA Ops:
  7.2 125.5 %copy-start = (bf16[312,600]{1,0:T(8,128)(2,1)S(1)}, bf16[312,600]{1,0:T(8,128)(2,1)}, u32[]{:S(2)}) copy-start(bf16[312,600]{1,0:T(8,128)(2,1)} %param.24) | copy-start | bytes 1123204
  7.2 120.9 %all-reduce.10.cloned.1.call-start = ((), (), s32[]{:S(2)}) async-start(), calls=%async_computation | async-start | bytes 2555904 | tf_op jit(solution)/shard_map/psum | solution.py:130
  17.4 6.4 copy-start.89
  23.8 54.7 %copy-start.26 = (bf16[156,312]{1,0:T(8,128)(2,1)S(1)}, bf16[156,312]{1,0:T(8,128)(2,1)}, u32[]{:S(2)}) copy-start(bf16[156,312]{1,0:T(8,128)(2,1)} %param.23) | copy-start | bytes 292036
  76.2 7.0 copy-start.1
  76.3 7.0 copy-start.34
  78.5 4.9 copy-start.85
  80.2 203.0 %all-reduce.12.cloned.1.call-start = ((), (), s32[]{:S(2)}) async-start(), calls=%async_computation.1 | async-start | bytes 2555904 | tf_op jit(solution)/shard_map/psum | solution.py:139
  83.3 49.3 %copy-start.81 = (f32[600]{0:T(1024)}, f32[600]{0:T(1024)S(1)}, u32[]{:S(2)}) copy-start(f32[600]{0:T(1024)S(1)} %convert_element_type.198) | copy-start | bytes 7204
  93.1 9.4 %copy-start.79 = (bf16[2,312]{1,0:T(2,128)(2,1)S(1)}, bf16[2,312]{1,0:T(2,128)(2,1)}, u32[]{:S(2)}) copy-start(bf16[2,312]{1,0:T(2,128)(2,1)} %param.28) | copy-start | bytes 3748
  93.1 10.0 %copy-start.61 = (bf16[2,312]{1,0:T(2,128)(2,1)S(1)}, bf16[2,312]{1,0:T(2,128)(2,1)}, u32[]{:S(2)}) copy-start(bf16[2,312]{1,0:T(2,128)(2,1)} %param.27) | copy-start | bytes 3748
  93.1 10.0 %copy-start.80 = (bf16[2,312]{1,0:T(2,128)(2,1)S(1)}, bf16[2,312]{1,0:T(2,128)(2,1)}, u32[]{:S(2)}) copy-start(bf16[2,312]{1,0:T(2,128)(2,1)} %param.29) | copy-start | bytes 3748
  103.1 44.1 %copy-start.53 = (f32[312]{0:T(512)}, f32[312]{0:T(512)S(1)}, u32[]{:S(2)}) copy-start(f32[312]{0:T(512)S(1)} %get-tuple-element.255) | copy-start | bytes 3748
  103.7 43.5 %copy-start.50 = (f32[312]{0:T(512)}, f32[312]{0:T(512)S(1)}, u32[]{:S(2)}) copy-start(f32[312]{0:T(512)S(1)} %get-tuple-element.253) | copy-start | bytes 3748
  103.7 43.5 %copy-start.63 = (f32[312]{0:T(512)}, f32[312]{0:T(512)S(1)}, u32[]{:S(2)}) copy-start(f32[312]{0:T(512)S(1)} %get-tuple-element.402) | copy-start | bytes 3748
  130.0 17.2 %copy-start.36 = (f32[2048]{0:T(1024)}, f32[2048]{0:T(1024)S(1)}, u32[]{:S(2)}) copy-start(f32[2048]{0:T(1024)S(1)} %broadcast_multiply_fusion.1) | copy-start | bytes 24580
  132.6 14.6 %copy-start.39 = (f32[2048]{0:T(1024)}, f32[2048]{0:T(1024)S(1)}, u32[]{:S(2)}) copy-start(f32[2048]{0:T(1024)S(1)} %fusion.160) | copy-start | bytes 24580
  132.7 16.0 %copy-start.87 = (bf16[600,312]{0,1:T(8,128)(2,1)S(1)}, bf16[600,312]{0,1:T(8,128)(2,1)}, u32[]{:S(2)}) copy-start(bf16[600,312]{0,1:T(8,128)(2,1)} %param.26) | copy-start | bytes 1123204
  150.9 219.0 %all-reduce.18.cloned.1.call-start = ((), (), s32[]{:S(2)}) async-start(), calls=%async_computation.4 | async-start | bytes 5111808 | tf_op jit(solution)/shard_map/psum | solution.py:130
  151.9 129.6 %copy-start.27 = (bf16[156,312]{1,0:T(8,128)(2,1)S(1)}, bf16[156,312]{1,0:T(8,128)(2,1)}, u32[]{:S(2)}) copy-start(bf16[156,312]{1,0:T(8,128)(2,1)} %param.23) | copy-start | bytes 292036
  283.2 5.5 slice-start.2
  283.2 5.5 slice-start.4
  288.7 88.2 %copy-start.46 = (f32[2048]{0:T(1024)}, f32[2048]{0:T(1024)S(1)}, u32[]{:S(2)}) copy-start(f32[2048]{0:T(1024)S(1)} %negate_multiply_fusion.3) | copy-start | bytes 24580
  296.7 316.5 %all-reduce.16.cloned.1.call-start = ((), (), s32[]{:S(2)}) async-start(), calls=%async_computation.3 | async-start | bytes 5111808 | tf_op jit(solution)/shard_map/psum | solution.py:139
  297.9 78.9 %copy-start.59 = (f32[312]{0:T(512)}, f32[312]{0:T(512)S(1)}, u32[]{:S(2)}) copy-start(f32[312]{0:T(512)S(1)} %get-tuple-element.259) | copy-start | bytes 3748
  371.9 5.0 copy-start.49
  371.9 6.4 copy-start.44
  384.8 5.9 copy-start.6
  448.4 5.9 copy-start.6
  509.5 6.2 copy-start.31
  512.6 10.0 %copy-start.24 = (bf16[3,312,156]{1,2,0:T(8,128)(2,1)S(1)}, bf16[3,312,156]{1,2,0:T(8,128)(2,1)}, u32[]{:S(2)}) copy-start(bf16[3,312,156]{1,2,0:T(8,128)(2,1)} %param.21) | copy-start | bytes 876100
  517.6 7.0 copy-start.5
  517.6 7.0 copy-start.14
  517.6 7.0 copy-start.45
  517.6 7.0 copy-start.55
  517.6 7.0 copy-start.58
  517.6 7.0 copy-start.60
  517.6 7.0 copy-start.65
  517.6 7.0 copy-start.83
  524.6 15.4 %copy-start.71 = (f32[312]{0:T(512)S(1)}, f32[312]{0:T(512)}, u32[]{:S(2)}) copy-start(f32[312]{0:T(512)} %get-tuple-element.248) | copy-start | bytes 3748
  524.6 15.4 %copy-start.70 = (f32[312]{0:T(512)S(1)}, f32[312]{0:T(512)}, u32[]{:S(2)}) copy-start(f32[312]{0:T(512)} %get-tuple-element.251) | copy-start | bytes 3748
  524.6 15.4 %copy-start.47 = (f32[2048]{0:T(1024)S(1)}, f32[2048]{0:T(1024)}, u32[]{:S(2)}) copy-start(f32[2048]{0:T(1024)} %copy-done.46) | copy-start | bytes 24580
  539.9 178.9 %all-reduce.14.cloned.1.call-start = ((), (), s32[]{:S(2)}) async-start(), calls=%async_computation.2 | async-start | bytes 5160960 | tf_op jit(solution)/shard_map/psum | solution.py:262
  551.6 65.5 %copy-start.15 = (bf16[2048,312]{0,1:T(8,128)(2,1)S(1)}, bf16[2048,312]{0,1:T(8,128)(2,1)}, u32[]{:S(2)}) copy-start(bf16[2048,312]{0,1:T(8,128)(2,1)} %get-tuple-element.333) | copy-start | bytes 3833860
  551.6 65.5 %copy-start.68 = (f32[312]{0:T(512)S(1)}, f32[312]{0:T(512)}, u32[]{:S(2)}) copy-start(f32[312]{0:T(512)} %get-tuple-element.258) | copy-start | bytes 3748
  613.2 6.8 copy-start.84
  617.1 66.8 %copy-start.57 = (f32[312]{0:T(512)S(1)}, f32[312]{0:T(512)}, u32[]{:S(2)}) copy-start(f32[312]{0:T(512)} %get-tuple-element.254) | copy-start | bytes 3748
  617.2 66.8 %copy-start.67 = (f32[312]{0:T(512)S(1)}, f32[312]{0:T(512)}, u32[]{:S(2)}) copy-start(f32[312]{0:T(512)} %get-tuple-element.403) | copy-start | bytes 3748
  (64 other events, 197.3 us)
Sparse Core Ops, SparseCore 0:
  80.3 47.7 all-reduce.9
  151.0 45.0 all-reduce.11
  296.8 73.0 all-reduce.17
  540.0 73.0 all-reduce.15
  617.6 101.1 all-reduce.13
where the time goes:
time: 740 us; the launch traced here: 733 us
  matrix products  229 us (31%)
  waiting for transfers between devices  190 us (26%)
  other arithmetic  169 us (23%)
  local copies, waits for them, and re-layouts  66.7 us (9%)
  blocking collectives  61.9 us (8%)
  between operations  15.2 us (2%)
    psum x2, waiting for transfers between devices, forward_pass(): lax.psum(partial_out.astype(jnp.bfloat16), 'tensor').astype(jnp.float32)  96.3 us
    sub x4, other arithmetic, attend_forward(): expo = jnp.exp(scores - peak)  66.4 us
    psum x1, blocking collectives, shards(): lax.psum((d_projection, d_offsets, d_combiner, d_expansion, d_thresholds,...  61.9 us
    psum x2, waiting for transfers between devices, forward_pass(): lax.psum(partial_down.astype(jnp.bfloat16), 'tensor').astype(jnp.float32)  61.5 us
    dot_general x12, matrix products, block_scores(): jnp.einsum('qhe,khe->hqk', query_block, keys, preferred_element_type=jnp....  51.1 us
    dot_general x8, matrix products, attend_forward(): jnp.einsum('hqk,khe->qhe', weights, values, preferred_element_type=jnp.fl...  45.2 us
    dot_general x4, matrix products, attend_backward(): jnp.einsum('qhe,khe->hqk', grad_block, values, preferred_element_type=jnp...  34.3 us
    convert_element_type x4, other arithmetic, attend_backward(): d_scores = (probs * (d_probs - delta)).astype(jnp.bfloat16)  33.6 us
  transfers between devices with their start and end apart: 5, of which 4 were waited for; matrix products, arithmetic and copies ran while one was open for 24% of the time, Pallas kernels for 0%

commit v1 on v0

v1 whole, which is shorter than its diff:
```python
import functools
import jax
import jax.numpy as jnp
from jax import lax
from jax.experimental import pallas as pl
from jax.experimental.pallas import tpu as pltpu
from jax.sharding import PartitionSpec as P

HEAD_DIM = 26
PAD = 32
EPS = 1e-05
MASKED = -1e30
SCALE = HEAD_DIM ** -0.5
LOG2E = 1.4426950408889634
BF = jnp.bfloat16
F32 = jnp.float32
NN = (((1,), (0,)), ((), ()))
NT = (((1,), (1,)), ((), ()))
TN = (((0,), (0,)), ((), ()))


def mm(a, b, dims=NN):
    return lax.dot_general(a, b, dims, preferred_element_type=F32)


def phi_pair(x):
    z = jnp.abs(x)
    t = 1.0 / (1.0 + (0.3275911 * 0.5 ** 0.5) * z)
    e = jnp.exp2(x * x * (-0.5 * LOG2E))
    poly = ((((1.061405429 * t - 1.453152027) * t + 1.421413741) * t - 0.284496736) * t + 0.254829592) * t
    tail = 0.5 * poly * e
    return jnp.where(x < 0, tail, 1.0 - tail), e * 0.3989422804014327


def body(
    tokens, cot, proj, offs, comb, up_in, thr_in, down_in, corr, gains, shifts, rows, cols, length,
    out_ref, dx_ref, dwt_ref, dcp_ref, dup_ref, ddown_ref, dsmall_ref,
    wt, cp, up, down, qkv, bias, probs, ctx32, ctx, inv, dctx, dxt, act, dgel, dpre, first_low, d_down, d_att, tok_aug, off_buf, rk_buf, ck_buf, k_buf, sem,
):
    T, D = tokens.shape
    shards = proj.shape[0]
    part = proj.shape[3]
    hs = part // HEAD_DIM
    heads = shards * hs
    width = hs * PAD
    hid = up_in.shape[2]
    hstride = up.shape[1] // shards
    BQ = 256

    r = lax.broadcasted_iota(jnp.int32, (width, part), 0)
    c = lax.broadcasted_iota(jnp.int32, (width, part), 1)
    inside = (r & (PAD - 1)) < HEAD_DIM
    sel = jnp.where(inside & (c == r - (PAD - HEAD_DIM) * (r >> 5)), 1.0, 0.0).astype(BF)
    up[...] = jnp.zeros_like(up)
    down[...] = jnp.zeros_like(down)
    for s in range(shards):
        for p in range(3):
            wt[pl.ds(p * heads * PAD + s * width, width), :] = mm(sel, proj[s, p], NT).astype(BF)
        cp[pl.ds(s * width, width), :] = mm(sel, comb[s]).astype(BF)
        up[:, s * hstride : s * hstride + hid] = up_in[s]
        down[s * hstride : s * hstride + hid, :] = down_in[s]
    tok_aug[...] = jnp.zeros_like(tok_aug)
    first_low[...] = jnp.zeros_like(first_low)
    tok_aug[:, 0:D] = tokens[...]
    ones = jnp.where(lax.broadcasted_iota(jnp.int32, (T, 128), 1) == D - 256, 1.0, 0.0).astype(BF)
    tok_aug[:, 256:384] = tok_aug[:, 256:384] + ones
    first_low[:, 256:384] = ones

    rr = lax.broadcasted_iota(jnp.int32, (width, 1), 0) & (PAD - 1)
    extra = jnp.where((rr == HEAD_DIM) | (rr == HEAD_DIM + 1), 1.0, 0.0)
    for s in range(shards):
        off = mm(sel, offs[s], NT)
        off_buf[s] = jnp.concatenate([off[:, 0:1], jnp.zeros((width, 1), F32), off[:, 1:2] + extra, jnp.zeros((width, 125), F32)], 1)

    def project(b, carry):
        t = pl.ds(pl.multiple_of(b * 256, 256), 256)
        for s in range(shards):
            for p in range(3):
                x = mm(wt[p * heads * PAD + s * width : p * heads * PAD + (s + 1) * width, :], tokens[t, :], NT)
                x = x + off_buf[s, :, p : p + 1]
                x = (x * (SCALE * LOG2E) if p == 0 else x).astype(BF)
                for h in range(hs):
                    qkv[p, s * hs + h, :, t] = x[h * PAD : (h + 1) * PAD, :]
        return carry

    lax.fori_loop(0, T // 256, project, 0)

    live = lax.broadcasted_iota(jnp.int32, (T, 128), 0) < length[...]
    rk_buf[...] = jnp.where(live, jnp.broadcast_to(rows[...].astype(F32), (128, T)).T, jnp.nan)
    ck_buf[...] = jnp.broadcast_to(cols[...].astype(F32), (128, T)).T

    def visible(j, carry):
        q = pl.ds(pl.multiple_of(j * 128, 128), 128)
        rq = rows[:, q].astype(F32)
        cq = cols[:, q].astype(F32)
        rk = rk_buf[...]
        gap = rk * (rk - rq) * rq * (ck_buf[...] - cq)
        bias[:, q] = jnp.where(gap == 0.0, 0.0, MASKED)
        return carry

    lax.fori_loop(0, T // 128, visible, 0)

    n, KC = T // BQ, 128

    def weigh(h):
        o = mm(qkv[2, h], probs[h])
        i = 1.0 / o[HEAD_DIM : HEAD_DIM + 1, :]
        inv[h] = i
        o = o * i
        ctx32[h] = o
        ctx[pl.ds(pl.multiple_of(h * PAD, PAD), PAD), :] = o.astype(BF)

    def forward_head(h, carry):
        peaks = [None] * n
        kept = {}
        k_buf[...] = qkv[1, h].T

        def score(j, c):
            q, r = slice(j * BQ, (j + 1) * BQ), slice(c * KC, (c + 1) * KC)
            s = mm(k_buf[r, :], qkv[0, h, :, q]) + bias[r, q]
            kept[j, c] = s
            m = jnp.max(s.reshape(KC // 8, 8, BQ), 0)
            peaks[j] = m if c == 0 else jnp.maximum(peaks[j], m)

        def expo(j, c):
            q, r = slice(j * BQ, (j + 1) * BQ), slice(c * KC, (c + 1) * KC)
            if c == 0:
                peaks[j] = jnp.max(peaks[j], 0, keepdims=True)
            probs[h, r, q] = jnp.exp2(kept.pop((j, c)) - peaks[j]).astype(BF)

        for j in range(n + 1):
            for c in range(T // KC):
                if j < n:
                    score(j, c)
                if j > 0:
                    expo(j - 1, c)
        weigh(h)
        return carry

    lax.fori_loop(0, heads, forward_head, 0)

    g0, g1 = gains[0:1, :].astype(F32), gains[1:2, :].astype(F32)
    b0, b1 = shifts[0:1, :].astype(F32), shifts[1:2, :].astype(F32)
    c0, c1 = corr[0:1, :].astype(F32), corr[1:2, :].astype(F32)
    thr = thr_in[...].astype(F32)
    dsmall_ref[...] = jnp.zeros_like(dsmall_ref)

    def norm(x):
        x = x - jnp.mean(x, -1, keepdims=True)
        rs = lax.rsqrt(jnp.mean(x * x, -1, keepdims=True) + EPS)
        return x * rs, rs

    def norm_back(dy, xhat, rs, g):
        d = dy * g
        return rs * (d - jnp.mean(d, -1, keepdims=True) - xhat * jnp.mean(d * xhat, -1, keepdims=True))

    def acc(i, v):
        dsmall_ref[i : i + 1, 0:D] += jnp.sum(v, 0, keepdims=True)

    BT = 256

    def middle(b, carry):
        t = pl.ds(pl.multiple_of(b * BT, BT), BT)
        att = mm(ctx[:, t], cp[...], TN)
        x1, rs1 = norm(tokens[t, :].astype(F32) + att + c0)
        first = x1 * g0 + b0
        low = first.astype(BF)
        first_low[t, 0:256] = low[:, 0:256]
        first_low[t, 256:D] = low[:, 256:D]
        ff = up.shape[1]
        dn = jnp.zeros((BT, D), F32)
        for j in range(ff // 256):
            u = slice(j * 256, (j + 1) * 256)
            pre = mm(low, up[:, u]) + thr[:, u]
            cdf, pdf = phi_pair(pre)
            a = (pre * cdf).astype(BF)
            act[t, u] = a
            dgel[:, u] = (cdf + pre * pdf).astype(BF)
            dn = dn + mm(a, down[u, :])
        x2, rs2 = norm(first + dn + c1)
        out_ref[t, :] = (x2 * g1 + b1).astype(BF)
        dy = cot[t, :].astype(F32)
        acc(0, dy * x2)
        acc(1, dy)
        dr2 = norm_back(dy, x2, rs2, g1)
        acc(2, dr2)
        dd = dr2.astype(BF)
        d_down[t, :] = dd
        df = dr2
        for j in range(ff // 256):
            u = slice(j * 256, (j + 1) * 256)
            dp = (mm(dd, down[u, :], NT) * dgel[:, u].astype(F32)).astype(BF)
            dpre[t, u] = dp
            df = df + mm(dp, up[:, u], NT)
        acc(3, df * x1)
        acc(4, df)
        dr1 = norm_back(df, x1, rs1, g0)
        acc(5, dr1)
        bias[t, 0:D] = dr1
        da = dr1.astype(BF)
        d_att[t, :] = da
        dctx[:, t] = mm(cp[...], da, NT).astype(BF)
        return carry

    lax.fori_loop(0, T // BT, middle, 0)

    def feed_grads(j, carry):
        u = pl.ds(pl.multiple_of(j * 256, 256), 256)
        ddown_ref[:, u] = mm(d_down[...], act[:, u], TN).astype(BF)
        dup_ref[:, u] = mm(first_low[:, 0 : dup_ref.shape[0]], dpre[:, u], TN).astype(BF)
        return carry

    lax.fori_loop(0, up.shape[1] // 256, feed_grads, 0)
    dcp_ref[...] = mm(ctx[...], d_att[...])

    def backward_head(h, carry):
        rowi = lax.broadcasted_iota(jnp.int32, (PAD, T), 0)
        hp = pl.ds(pl.multiple_of(h * PAD, PAD), PAD)
        i = inv[h]
        do = dctx[hp, :].astype(F32)
        nd = jnp.sum(do * ctx32[h], 0, keepdims=True) * (-i)
        hi = nd.astype(BF).astype(F32)
        da = jnp.where(rowi == HEAD_DIM, hi, jnp.where(rowi == HEAD_DIM + 1, nd - hi, do * i)).astype(BF)
        kt = qkv[1, h]
        vt = qkv[2, h]
        qt = qkv[0, h]
        v = vt.T
        hp2 = pl.ds(pl.multiple_of((2 * heads + h) * PAD, PAD), PAD)
        hp1 = pl.ds(pl.multiple_of((heads + h) * PAD, PAD), PAD)
        dq = jnp.zeros((PAD, T), F32)
        for j in range(T // BQ):
            r = slice(j * BQ, (j + 1) * BQ)
            pk = probs[h, r, :]
            dxt[hp2, r] = mm(da, pk, NT).astype(BF)
            ds = (pk.astype(F32) * mm(v[r], da)).astype(BF)
            dxt[hp1, r] = (mm(qt, ds, NT) * (1.0 / LOG2E)).astype(BF)
            dq = dq + mm(kt[:, r], ds)
        dxt[hp, :] = (dq * SCALE).astype(BF)
        return carry

    lax.fori_loop(0, heads, backward_head, 0)

    def weight_grads(p, carry):
        w = pl.ds(pl.multiple_of(p * heads * PAD, PAD), heads * PAD)
        dwt_ref[w, :] = mm(dxt[w, :], tok_aug[...])
        return carry

    lax.fori_loop(0, 3, weight_grads, 0)

    def input_grads(b, carry):
        t = pl.ds(pl.multiple_of(b * BT, BT), BT)
        bias[t, 0:D] = bias[t, 0:D] + mm(dxt[:, t], wt[...], TN)
        return carry

    lax.fori_loop(0, T // BT, input_grads, 0)
    put = pltpu.make_async_copy(bias.at[:, 0:384], dx_ref, sem)
    put.start()
    put.wait()


def compute(tokens, cot, proj, offs, comb, up, thr, down, corr, gains, shifts, rows, cols, length):
    T, D = tokens.shape
    shards, hs = proj.shape[0], proj.shape[3] // HEAD_DIM
    heads = shards * hs
    W = heads * PAD
    FFP = thr.shape[1]
    outs = (
        jax.ShapeDtypeStruct((T, D), BF),
        jax.ShapeDtypeStruct((T, 384), F32),
        jax.ShapeDtypeStruct((3 * W, 384), F32),
        jax.ShapeDtypeStruct((W, D), F32),
        jax.ShapeDtypeStruct((320, FFP), BF),
        jax.ShapeDtypeStruct((D, FFP), BF),
        jax.ShapeDtypeStruct((8, 384), F32),
    )
    ins = (tokens, cot, proj, offs, comb, up, thr, down, corr, gains, shifts, rows, cols, length)
    V = pltpu.VMEM
    scratch = [
        V((3 * W, D), BF), V((W, D), BF), V((D, FFP), BF), V((FFP, D), BF),
        V((3, heads, PAD, T), BF), V((T, T), F32), V((heads, T, T), BF),
        V((heads, PAD, T), F32), V((W, T), BF), V((heads, 1, T), F32), V((W, T), BF), V((3 * W, T), BF),
        V((T, FFP), BF), V((256, FFP), BF), V((T, FFP), BF), V((T, 384), BF), V((T, D), BF), V((T, D), BF), V((T, 384), BF), V((shards, hs * PAD, 128), F32), V((T, 128), F32), V((T, 128), F32), V((T, PAD), BF), pltpu.SemaphoreType.DMA(()),
    ]
    vm = pl.BlockSpec(memory_space=pltpu.VMEM)
    return pl.pallas_call(
        body, out_shape=outs, in_specs=[vm] * len(ins), out_specs=(vm, pl.BlockSpec(memory_space=pl.ANY)) + (vm,) * (len(outs) - 2), scratch_shapes=scratch,
        compiler_params=pltpu.CompilerParams(vmem_limit_bytes=63 * 2 ** 20),
    )(*ins)


def shards(tokens, projection, offsets, combiner, expansion, thresholds, contraction, corrections, gains, shifts, table_rows, table_columns, table_lengths, cotangent):
    two = table_lengths.shape[0]
    T, D = tokens.shape[0] // two, tokens.shape[1]
    part, hid = projection.shape[2], thresholds.shape[0]
    hstride = -(-hid // 128) * 128
    me = lax.axis_index("tensor")
    swap = [(0, 1), (1, 0)]

    def other(x):
        return lax.ppermute(x, "tensor", swap)

    def mine(x):
        return lax.dynamic_index_in_dim(x.reshape((two, T) + x.shape[1:]), me, 0, keepdims=False)

    def pair(x):
        return jnp.stack((x, other(x)))

    offs = jnp.pad(pair(offsets), ((0, 0), (0, 6), (0, 0)))
    thr = jnp.pad(pair(thresholds), ((0, 0), (0, hstride - hid))).reshape(1, two * hstride)
    length = lax.dynamic_slice_in_dim(table_lengths, me, 1).reshape(1, 1)
    out, dx, dwt, dcp, dup, ddown, small = compute(
        mine(tokens), mine(cotangent), pair(projection), offs, pair(combiner), pair(expansion), thr, pair(contraction),
        corrections, gains, shifts, mine(table_rows).reshape(1, T), mine(table_columns).reshape(1, T), length,
    )

    def whole(x):
        y = other(x)
        return jnp.where(me == 0, jnp.concatenate((x, y)), jnp.concatenate((y, x)))

    def reduced(x):
        return lax.psum(x[0].astype(F32) + other(x[1].astype(BF)).astype(F32), "dp")

    hs = part // HEAD_DIM
    dwt = dwt.reshape(3, two, hs, PAD, 384)[:, :, :, :HEAD_DIM, : D + 1].transpose(1, 0, 2, 3, 4).reshape(two, 3, part, D + 1)
    dwt = reduced(dwt)
    dcp = reduced(dcp.reshape(two, hs, PAD, D)[:, :, :HEAD_DIM].reshape(two, part, D))
    dup = reduced(dup.reshape(320, two, hstride)[: D + 1, :, :hid].transpose(1, 0, 2))
    ddown = reduced(ddown.reshape(D, two, hstride)[:, :, :hid].transpose(1, 0, 2))
    small = lax.psum(small, ("dp", "tensor"))[:, :D]
    return (
        whole(out),
        whole(dx[:, :D].astype(BF)).astype(F32),
        dwt[:, :, :D].transpose(0, 2, 1),
        jnp.stack((dwt[0, :, D], dwt[2, :, D])),
        dcp,
        dup[:D],
        dup[D],
        ddown.T,
        jnp.stack((small[5], small[2])),
        jnp.stack((small[3], small[0])),
        jnp.stack((small[4], small[1])),
    )


def solution(mesh):
    return jax.shard_map(
        shards,
        mesh=mesh,
        in_specs=(
            P("dp", None), P(None, None, "tensor"), P(None, "tensor"), P("tensor", None), P(None, "tensor"), P("tensor"),
            P("tensor", None), P(), P(), P(), P("dp"), P("dp"), P("dp"), P("dp", None),
        ),
        out_specs=(
            P("dp", None), P("dp", None), P(None, None, "tensor"), P(None, "tensor"), P("tensor", None), P(None, "tensor"),
            P("tensor"), P("tensor", None), P(), P(), P(),
        ),
        check_vma=False,
    )
```

time: 740 us -> 300 us (0.41)
  matrix products: 229 us -> 0 us
  other arithmetic: 169 us -> 19.5 us
  waiting for transfers between devices: 190 us -> 76.5 us
  Pallas kernels: 0 us -> 85.2 us
  local copies, waits for them, and re-layouts: 66.7 us -> 40.3 us
  starting transfers between devices: 0.2 us -> 13.8 us
  blocking collectives: 61.9 us -> 49.1 us
    dot_general x51 -> x0, matrix products: 229 us -> none  [the longest x12 51.1 us: block_scores(): jnp.einsum('qhe,khe->hqk', query_block, keys, preferred_element_type=jnp....]
    psum x5 -> x1, waiting for transfers between devices: 189 us -> 35.2 us  [reduced(): return lax.psum(x[0].astype(F32) + other(x[1].astype(BF)).astype(F32), 'dp')]
    pallas_call x0 -> x1, Pallas kernels: none -> 85.2 us  [compute(): pl.pallas_call(body, out_shape=outs, in_specs=[vm] * len(ins), out_specs=...]
    sub x4 -> x0, other arithmetic: 66.4 us -> none  [attend_forward(): expo = jnp.exp(scores - peak)]
    convert_element_type x11 -> x1, other arithmetic: 44.7 us -> 2.34 us  [shards(): whole(dx[:, :D].astype(BF)).astype(F32)]
    ppermute x0 -> x12, waiting for transfers between devices: none -> 41.3 us  [other(): return lax.ppermute(x, 'tensor', swap)]
    reduce_sum x18 -> x0, other arithmetic: 40.4 us -> none  [the longest x4 14.4 us: attend_forward(): summed = jnp.sum(expo, -1, keepdims=True)]
    ppermute x0 -> x12, starting transfers between devices: none -> 13.8 us  [other(): return lax.ppermute(x, 'tensor', swap)]
  transfers between devices with their start and end apart: 5 -> 13, of which waited for: 4 -> 5; matrix products, arithmetic and copies ran while one was open for 24% -> 15% of each run, Pallas kernels for 0% -> 0%
where the time goes in v1:
time: 300 us; the launch traced here: 299 us
  Pallas kernels  85.2 us (28%)
  waiting for transfers between devices  76.5 us (26%)
  blocking collectives  49.1 us (16%)
  local copies, waits for them, and re-layouts  40.3 us (13%)
  other arithmetic  19.5 us (6%)
  between operations  14.3 us (5%)
  starting transfers between devices  13.8 us (5%)
    pallas_call x1, Pallas kernels, compute(): pl.pallas_call(body, out_shape=outs, in_specs=[vm] * len(ins), out_specs=...  85.2 us
    psum x1, blocking collectives, shards(): small = lax.psum(small, ('dp', 'tensor'))[:, :D]  49.1 us
    ppermute x12, waiting for transfers between devices, other(): return lax.ppermute(x, 'tensor', swap)  41.3 us
    psum x1, waiting for transfers between devices, reduced(): return lax.psum(x[0].astype(F32) + other(x[1].astype(BF)).astype(F32), 'dp')  35.2 us
    ppermute x12, starting transfers between devices, other(): return lax.ppermute(x, 'tensor', swap)  13.8 us
    unnamed x33, local copies, waits for them, and re-layouts  10.7 us
    another operation x5, other arithmetic, pair(): return jnp.stack((x, other(x)))  7.38 us
  transfers between devices with their start and end apart: 13, of which 5 were waited for; matrix products, arithmetic and copies ran while one was open for 15% of the time, Pallas kernels for 0%

profile of v1, /device:TPU:0, one launch (start us, length us, event | category | flops | bytes accessed | tf_op | source)
XLA Modules:
  0.0 298.9 jit_solution(6800474456099110688)
XLA Ops:
  7.2 3.0 %collective-permute-start.1 = (bf16[2,156]{1,0:T(2,128)(2,1)}, bf16[2,156]{1,0:T(2,128)(2,1)}, u32[]{:S(2)}, u32[]{:S(2)}) collective-permute-start(bf16[2,156]{1,0:T(2,128)(2,1)} %param.16), channel_id=1, source_target_pairs={{0,1},{1,0},{2,3},{3,2},{4,5},{5,4},{6,7},{7,6},{8,9},{9,8},{10,11... | collective-permute-start | bytes 1880 | tf_op jit(solution)/shard_map/ppermute | solution.py:300
  10.3 1.9 collective-permute-start.2
  12.4 2.0 copy.50
  14.3 1.9 collective-permute-start.5
  17.0 1.3 reshape.74
  18.3 1.8 copy.63
  20.1 1.8 copy.64
  22.0 1.3 dynamic-slice_bitcast_fusion
  24.5 1.3 copy.48
  25.9 1.3 fusion.4.offs
  28.5 1.7 pad_maximum_fusion.3.comb
  30.2 13.9 %collective-permute-done = bf16[3,312,156]{2,1,0:T(8,128)(2,1)S(1)} collective-permute-done((bf16[3,312,156]{2,1,0:T(8,128)(2,1)S(1)}, bf16[3,312,156]{2,1,0:T(8,128)(2,1)S(1)}, u32[]{:S(2)}, u32[]{:S(2)}) %collective-permute-start) | collective-permute-done | bytes 292064 | tf_op jit(solution)/shard_map/ppermute | solution.py:300
  44.1 1.1 pad_maximum_fusion.proj
  45.2 1.0 pad_maximum_fusion.2.up_in
  46.2 2.3 pad_maximum_fusion.1.down_in
  48.5 85.2 %shard_map.221 = (bf16[1024,312]{1,0:T(8,128)(2,1)}, f32[1024,384]{1,0:T(8,128)}, f32[1152,384]{1,0:T(8,128)}, f32[384,312]{1,0:T(8,128)}, bf16[320,1280]{1,0:T(...) custom-call(bf16[1024,312]{1,0:T(8,128)(2,1)} %get-tuple-element.71.tokens, ...), custom_call_target="tpu_custom_call" | custom-call | tf_op jit(solution)/shard_map/pallas_call | solution.py:285
  133.8 1.0 slice.149
  134.8 1.0 slice.116
  135.7 1.6 copy_bitcast_fusion
  138.2 1.6 collective-permute-start.9
  139.9 0.9 convert_element_type.41
  141.2 1.1 copy.52
  142.3 1.6 collective-permute-start.6
  144.2 0.8 slice_bitcast_fusion.3
  145.4 2.1 reshape.78
  148.2 1.7 collective-permute-start.10
  149.9 0.7 convert_add_fusion.3
  150.6 2.0 collective-permute-done.8
  152.6 1.9 convert_add_fusion.2
  154.6 20.3 %collective-permute-done.11 = bf16[312,600]{1,0:T(8,128)(2,1)} collective-permute-done((bf16[312,600]{1,0:T(8,128)(2,1)}, bf16[312,600]{1,0:T(8,128)(2,1)}, u32[]{:S(2)}, u32[]{:S(2)}) %collective-permute-start.11) | collective-permute-done | bytes 374432 | tf_op jit(solution)/shard_map/ppermute | solution.py:300
  174.9 2.0 fusion.1
  176.8 5.1 %collective-permute-done.10 = bf16[313,600]{1,0:T(8,128)(2,1)S(1)} collective-permute-done((bf16[313,600]{1,0:T(8,128)(2,1)S(1)}, bf16[313,600]{1,0:T(8,128)(2,1)S(1)}, u32[]{:S(2)}, u32[]{:S(2)}) %collective-permute-start.10) | collective-permute-done | bytes 375632 | tf_op jit(solution)/shard_map/ppermute | solution.py:300
  181.9 1.0 convert_add_fusion
  183.0 1.4 copy-done.6
  184.4 1.1 copy.55
  185.5 0.9 collective-permute-start.7
  186.4 49.1 %psum.39 = f32[8,384]{1,0:T(8,128)S(1)} all-reduce(f32[8,384]{1,0:T(8,128)S(1)} %copy-done.9), channel_id=1, replica_groups=mesh['dp'=16,'tensor'=2] {'dp','tensor'}, use_global_device_ids=true, to_apply=%region_4.5 | all-reduce | flops 3072 | bytes 24576 | tf_op jit(solution)/shard_map/psum | solution.py:329
  237.3 2.2 copy.53
  239.5 1.8 maximum_select_fusion
  241.4 1.5 copy.61
  242.9 2.2 copy.56
  245.2 2.3 fusion
  247.5 2.2 copy.62
  249.7 35.2 %all-reduce.5.cloned.1.call-done = (f32[3,156,313]{2,1,0:T(8,128)}, f32[156,312]{1,0:T(8,128)}, f32[313,600]{1,0:T(8,128)}, f32[600,312]{0,1:T(8,128)}) async-done(((f32[3,156,313]{2,1,0:T(8,128)}, f32[156,312]{1,0:T(8,128)}, f32[313,600]{1,0:T(8,128)}, f32[600,312]{0,1:T(8,128)}), (f32[3,156,313]{2,1,0:T(8,128)}, f32[156,312]{1,0:T(8,128)}, f32[313,600]{1,0:T(8,128)}, ...) | async-done | bytes 2280640 | tf_op jit(solution)/shard_map/psum | solution.py:321
  284.9 1.2 slice_reduce_fusion.1
  286.2 2.1 slice_bitcast_fusion
  288.9 0.9 slice.121
  291.1 0.9 copy.79
  (63 shorter events, 10.1 us)
Async XLA Ops:
  7.2 277.8 %all-reduce.5.cloned.1.call-start = ((), (), s32[]{:S(2)}) async-start(), calls=%async_computation | async-start | bytes 5201920 | tf_op jit(solution)/shard_map/psum | solution.py:321
  7.2 18.6 %collective-permute-start.1 = (bf16[2,156]{1,0:T(2,128)(2,1)}, bf16[2,156]{1,0:T(2,128)(2,1)}, u32[]{:S(2)}, u32[]{:S(2)}) collective-permute-start(bf16[2,156]{1,0:T(2,128)(2,1)} %param.16), channel_id=1, source_target_pairs={{0,1},{1,0},{2,3},{3,2},{4,5},{5,4},{6,7},{7,6},{8,9},{9,8},{10,11... | collective-permute-start | bytes 1880 | tf_op jit(solution)/shard_map/ppermute | solution.py:300
  10.3 17.0 %collective-permute-start.4 = (bf16[600]{0:T(1024)(128)(2,1)}, bf16[600]{0:T(1024)(128)(2,1)}, u32[]{:S(2)}, u32[]{:S(2)}) collective-permute-start(bf16[600]{0:T(1024)(128)(2,1)} %param.19), channel_id=1, source_target_pairs={{0,1},{1,0},{2,3},{3,2},{4,5},{5,4},{6,7},{7,6},{8,9},{9,8},{10,11... | collective-permute-start | bytes 3608 | tf_op jit(solution)/shard_map/ppermute | solution.py:300
  10.3 18.2 %collective-permute-start.2 = (bf16[156,312]{1,0:T(8,128)(2,1)}, bf16[156,312]{1,0:T(8,128)(2,1)}, u32[]{:S(2)}, u32[]{:S(2)}) collective-permute-start(bf16[156,312]{1,0:T(8,128)(2,1)} %param.17), channel_id=1, source_target_pairs={{0,1},{1,0},{2,3},{3,2},{4,5},{5,4},{6,7},{7,6},{8,9},{9,8},{10,11... | collective-permute-start | bytes 292040 | tf_op jit(solution)/shard_map/ppermute | solution.py:300
  12.3 32.9 %collective-permute-start.3 = (bf16[312,600]{1,0:T(8,128)(2,1)}, bf16[312,600]{1,0:T(8,128)(2,1)S(1)}, u32[]{:S(2)}, u32[]{:S(2)}) collective-permute-start(bf16[312,600]{1,0:T(8,128)(2,1)} %param.18), channel_id=1, source_target_pairs={{0,1},{1,0},{2,3},{3,2},{4,5},{5,4},{6,7},{7,6},{8,9},{9,8},{10,11... | collective-permute-start | bytes 1123208 | tf_op jit(solution)/shard_map/ppermute | solution.py:300
  14.3 31.9 %collective-permute-start.5 = (bf16[600,312]{1,0:T(8,128)(2,1)}, bf16[600,312]{1,0:T(8,128)(2,1)}, u32[]{:S(2)}, u32[]{:S(2)}) collective-permute-start(bf16[600,312]{1,0:T(8,128)(2,1)} %copy.50), channel_id=1, source_target_pairs={{0,1},{1,0},{2,3},{3,2},{4,5},{5,4},{6,7},{7,6},{8,9},{9,8},{10,11... | collective-permute-start | bytes 1123208 | tf_op jit(solution)/shard_map/ppermute | solution.py:300
  21.9 1.4 copy-start.8
  22.0 2.0 copy-start.10
  22.0 2.0 copy-start.11
  24.5 20.7 %copy-start.5 = (bf16[312,600]{1,0:T(8,128)(2,1)S(1)}, bf16[312,600]{1,0:T(8,128)(2,1)}, u32[]{:S(2)}) copy-start(bf16[312,600]{1,0:T(8,128)(2,1)} %param.18) | copy-start | bytes 1123204
  25.8 18.3 %collective-permute-start = (bf16[3,312,156]{2,1,0:T(8,128)(2,1)S(1)}, bf16[3,312,156]{2,1,0:T(8,128)(2,1)S(1)}, u32[]{:S(2)}, u32[]{:S(2)}) collective-permute-start(bf16[3,312,156]{2,1,0:T(8,128)(2,1)S(1)} %copy.48), channel_id=1, source_target_pairs={{0,1},{1,0},{2,3},{3,2},{4,5},{5,4},{6,7},{7,6},{8,9},{9,8},{10,11... | collective-permute-start | bytes 876104 | tf_op jit(solution)/shard_map/ppermute | solution.py:300
  137.5 3.8 %copy-start.1 = (bf16[1024,312]{1,0:T(8,128)(2,1)S(1)}, bf16[1024,312]{1,0:T(8,128)(2,1)}, u32[]{:S(2)}) copy-start(bf16[1024,312]{1,0:T(8,128)(2,1)} %get-tuple-element.18) | copy-start | bytes 1916932
  138.2 11.7 %collective-permute-start.9 = (bf16[156,312]{1,0:T(8,128)(2,1)}, bf16[156,312]{1,0:T(8,128)(2,1)S(1)}, u32[]{:S(2)}, u32[]{:S(2)}) collective-permute-start(bf16[156,312]{1,0:T(8,128)(2,1)} %convert_element_type.43), channel_id=1, source_target_pairs={{0,1},{1,0},{2,3},{3,2},{4,5},{5,4},{6,7},{7,6},{8,9},{9,8},{10,11... | collective-permute-start | bytes 292040 | tf_op jit(solution)/shard_map/ppermute | solution.py:300
  139.9 4.0 %copy-start.3 = (bf16[312,1280]{1,0:T(8,128)(2,1)S(1)}, bf16[312,1280]{1,0:T(8,128)(2,1)}, u32[]{:S(2)}) copy-start(bf16[312,1280]{1,0:T(8,128)(2,1)} %get-tuple-element.23) | copy-start | bytes 2396164
  140.8 11.8 %collective-permute-start.8 = (bf16[3,156,313]{2,1,0:T(8,128)(2,1)}, bf16[3,156,313]{2,1,0:T(8,128)(2,1)}, u32[]{:S(2)}, u32[]{:S(2)}) collective-permute-start(bf16[3,156,313]{2,1,0:T(8,128)(2,1)} %convert_element_type.41), channel_id=1, source_target_pairs={{0,1},{1,0},{2,3},{3,2},{4,5},{5,4},{6,7},{7,6},{8,9},{9,8},{10,11... | collective-permute-start | bytes 878912 | tf_op jit(solution)/shard_map/ppermute | solution.py:300
  142.3 95.0 %collective-permute-start.6 = (bf16[1024,312]{0,1:T(8,128)(2,1)}, bf16[1024,312]{0,1:T(8,128)(2,1)}, u32[]{:S(2)}, u32[]{:S(2)}) collective-permute-start(bf16[1024,312]{0,1:T(8,128)(2,1)} %copy.52), channel_id=1, source_target_pairs={{0,1},{1,0},{2,3},{3,2},{4,5},{5,4},{6,7},{7,6},{8,9},{9,8},{10,11... | collective-permute-start | bytes 1916936 | tf_op jit(solution)/shard_map/ppermute | solution.py:300
  145.0 29.9 %collective-permute-start.11 = (bf16[312,600]{1,0:T(8,128)(2,1)}, bf16[312,600]{1,0:T(8,128)(2,1)}, u32[]{:S(2)}, u32[]{:S(2)}) collective-permute-start(bf16[312,600]{1,0:T(8,128)(2,1)} %slice_bitcast_fusion.3), channel_id=1, source_target_pairs={{0,1},{1,0},{2,3},{3,2},{4,5},{5,4},{6,7},{7,6},{8,9},{9,8},{10,11... | collective-permute-start | bytes 1123208 | tf_op jit(solution)/shard_map/ppermute | solution.py:300
  148.2 33.7 %collective-permute-start.10 = (bf16[313,600]{1,0:T(8,128)(2,1)S(1)}, bf16[313,600]{1,0:T(8,128)(2,1)S(1)}, u32[]{:S(2)}, u32[]{:S(2)}) collective-permute-start(bf16[313,600]{1,0:T(8,128)(2,1)S(1)} %slice_bitcast_fusion.1), channel_id=1, source_target_pairs={{0,1},{1,0},{2,3},{3,2},{4,5},{5,4},{6,7},{7,6},{8,9},{9,8},{10,11... | collective-permute-start | bytes 1126808 | tf_op jit(solution)/shard_map/ppermute | solution.py:300
  182.9 1.4 copy-start.6
  182.9 3.5 %copy-start.9 = (f32[8,384]{1,0:T(8,128)S(1)}, f32[8,384]{1,0:T(8,128)}, u32[]{:S(2)}) copy-start(f32[8,384]{1,0:T(8,128)} %get-tuple-element.24) | copy-start | bytes 36868
  184.4 57.0 %copy-start = (bf16[1024,312]{1,0:T(8,128)(2,1)}, bf16[1024,312]{1,0:T(8,128)(2,1)S(1)}, u32[]{:S(2)}) copy-start(bf16[1024,312]{1,0:T(8,128)(2,1)S(1)} %slice.147) | copy-start | bytes 1916932
  185.5 57.4 %collective-permute-start.7 = (bf16[1024,312]{0,1:T(8,128)(2,1)}, bf16[1024,312]{0,1:T(8,128)(2,1)}, u32[]{:S(2)}, u32[]{:S(2)}) collective-permute-start(bf16[1024,312]{0,1:T(8,128)(2,1)} %copy.55), channel_id=1, source_target_pairs={{0,1},{1,0},{2,3},{3,2},{4,5},{5,4},{6,7},{7,6},{8,9},{9,8},{10,11... | collective-permute-start | bytes 1916936 | tf_op jit(solution)/shard_map/ppermute | solution.py:300
  284.9 3.4 %copy-start.4 = (f32[313,600]{1,0:T(8,128)S(1)}, f32[313,600]{1,0:T(8,128)}, u32[]{:S(2)}) copy-start(f32[313,600]{1,0:T(8,128)} %get-tuple-element.62) | copy-start | bytes 2253604
  286.2 4.3 %copy-start.7 = (f32[156,312]{1,0:T(8,128)S(1)}, f32[156,312]{1,0:T(8,128)}, u32[]{:S(2)}) copy-start(f32[156,312]{1,0:T(8,128)} %get-tuple-element.78) | copy-start | bytes 584068
  286.2 5.0 %copy-start.2 = (f32[600,312]{0,1:T(8,128)S(1)}, f32[600,312]{0,1:T(8,128)}, u32[]{:S(2)}) copy-start(f32[600,312]{0,1:T(8,128)} %get-tuple-element.81) | copy-start | bytes 2246404
Sparse Core Ops, SparseCore 0:
  183.1 101.8 all-reduce.4

commit v2 on v1

v2 whole, which is shorter than its diff:
```python
import functools

import jax
import jax.numpy as jnp
from jax import lax
from jax.experimental import pallas as pl
from jax.experimental.pallas import tpu as pltpu
from jax.sharding import PartitionSpec as P

HEAD_DIM = 26
PAD = 32
TRIPLE = 3 * PAD
EPS = 1e-05
MASKED = -1e30
SCALE = HEAD_DIM ** -0.5
LOG2E = 1.4426950408889634
BF = jnp.bfloat16
F32 = jnp.float32
NN = (((1,), (0,)), ((), ()))
NT = (((1,), (1,)), ((), ()))
TN = (((0,), (0,)), ((), ()))
BT = 256
MESH = pl.DeviceIdType.MESH


def mm(a, b, dims=NN):
    return lax.dot_general(a, b, dims, preferred_element_type=F32)


def up_to(x, m):
    return -(-x // m) * m


def wide(x):
    return jnp.concatenate([x, x], 1)


def phi_pair(x):
    z = jnp.abs(x)
    t = 1.0 / (1.0 + (0.3275911 * 0.5 ** 0.5) * z)
    e = jnp.exp2(x * x * (-0.5 * LOG2E))
    poly = ((((0.5307027145 * t - 0.7265760135) * t + 0.7107068705) * t - 0.142248368) * t + 0.127414796) * t
    tail = poly * e
    return jnp.where(x < 0, tail, 1.0 - tail), e * 0.3989422804014327


def selector(hs):
    r = lax.broadcasted_iota(jnp.int32, (hs * PAD, hs * HEAD_DIM), 0)
    c = lax.broadcasted_iota(jnp.int32, (hs * PAD, hs * HEAD_DIM), 1)
    inside = (r & (PAD - 1)) < HEAD_DIM
    return jnp.where(inside & (c == r - (PAD - HEAD_DIM) * (r >> 5)), 1.0, 0.0).astype(BF)


INPUTS = (
    "tok_in", "cot_in", "proj_in", "comb_in", "up_in", "down_in", "thr_in", "offs_in", "corr_in", "gain_in", "shift_in", "rows_in", "cols_in", "len_in",
)


class Plan:
    def __init__(self, n, hs):
        feed, out = 5 * 160, 5 * (hs * PAD // 4)
        self.parts = PARTS
        self.down, self.up, self.comb, self.small = (0, 0), (1, 0), (1, feed), (1, feed + out)
        self.used = [feed, feed + out + 48] + [5 * (hp * TRIPLE // 4) for hp in self.parts]
        self.first_part = 2
        chain, left = [], n
        while left > 1:
            chain.append(min(4, left))
            left //= chain[-1]
        self.levels = [([n], False) if flat and n <= 8 else (chain, True) for flat in FLAT]
        self.rows = []
        for x, (sizes, swap) in zip(self.used, self.levels):
            cut = 1
            for z in sizes[:-1] if swap else sizes:
                cut *= z
            self.rows.append(up_to(x, 16 * cut))
        self.schedule = SCHEDULE
        self.after = AFTER

    def blocks(self, g):
        sizes, swap = self.levels[g]
        out = [self.rows[g]]
        for j, z in enumerate(sizes):
            out.append(out[-1] if swap and j == len(sizes) - 1 else out[-1] // z)
        return out


PARTS = (4, 2)
FLAT = (False, False, False, True)
SCHEDULE = {0: [(0, 2)], 1: [(1, 2)], 3: [(0, 3)], 5: [(0, 4), (1, 3)], 7: ["part0", (2, 1), (0, 5), (1, 4)], 8: [(2, 2)], 9: [(0, 6), (1, 5)], 10: [(2, 3), (0, 7)], 11: [(1, 6), (2, 4)]}
AFTER = [(3, 1), "w", 0, (3, 2), "send", 1, (1, 7), (2, 5), 2, (3, 3), 3, (2, 6), (3, 4), (2, 7), (3, 5), (3, 6)]


def main_kernel(n, hs, plan, names, *refs):
    r = dict(zip(names, refs))
    tok_in, cot_in, proj_in, comb_in, up_in, down_in, thr_in, offs_in, corr_in, gain_in, shift_in, rows_in, cols_in, len_in = (r[k] for k in INPUTS)
    lo_out, dxo_out, dxp_out = r["lo_out"], r["dxo_out"], r["dxp_out"]
    tok, cot, first_low, d_down, d_att = (r[k] for k in ("tok", "cot", "first_low", "d_down", "d_att"))
    raw_proj, raw_comb, raw_up, raw_down = (r[k] for k in ("raw_proj", "raw_comb", "raw_up", "raw_down"))
    raw_thr, raw_offs, raw_corr, raw_gain, raw_shift = (r[k] for k in ("raw_thr", "raw_offs", "raw_corr", "raw_gain", "raw_shift"))
    wt, cp, cpt, upt, downn = (r[k] for k in ("wt", "cp", "cpt", "upt", "downn"))
    qkv, bias, probs, ctx32, ctx, inv, dctx, dxt, dpre = (
        r[k] for k in ("qkv", "bias", "probs", "ctx32", "ctx", "inv", "dctx", "dxt", "dpre")
    )
    vbuf, thr_buf, off_buf, acc, k_buf = (r[k] for k in ("vbuf", "thr_buf", "off_buf", "acc", "k_buf"))
    rows, cols, lsem, wsend, wrecv, gsend, grecv, gloc, osend, orecv, xsend, xrecv = (
        r[k] for k in ("rows", "cols", "lsem", "wsend", "wrecv", "gsend", "grecv", "gloc", "osend", "orecv", "xsend", "xrecv")
    )
    act = dxt
    D, T = tok.shape
    heads = 2 * hs
    part = hs * HEAD_DIM
    width = hs * PAD
    srows = hs * TRIPLE
    hid = up_in.shape[1]
    hst = upt.shape[0] // 2

    me, dp = lax.axis_index("tensor"), lax.axis_index("dp")
    core, chip = lax.rem(dp, 2), lax.div(dp, 2)
    peer = {"tensor": 1 - me}
    sib = {"dp": dp + 1 - 2 * core}

    def chip_at(k):
        return lax.rem(chip + k, n)

    def on_chip(k):
        return {"dp": chip_at(k) * 2 + core}

    def remote(src, dst, ssem, rsem, dev):
        return pltpu.make_async_remote_copy(src_ref=src, dst_ref=dst, send_sem=ssem, recv_sem=rsem, device_id=dev, device_id_type=MESH)

    mine = pl.ds(pl.multiple_of(me * T, T), T)
    mine8 = pl.ds(pl.multiple_of(me * (T // 128), T // 128), T // 128)
    loads = {}
    for i, (k, a, b) in enumerate((
        ("proj", proj_in, raw_proj.at[0]), ("offs", offs_in, raw_offs.at[0]), ("tok", tok_in.at[:, mine], tok), ("rows", rows_in.at[mine8, :], rows),
        ("cols", cols_in.at[mine8, :], cols), ("comb", comb_in, raw_comb.at[0]), ("up", up_in, raw_up.at[0]), ("down", down_in, raw_down.at[0]),
        ("thr", thr_in, raw_thr.at[0]), ("corr", corr_in, raw_corr), ("gain", gain_in, raw_gain), ("shift", shift_in, raw_shift), ("cot", cot_in.at[:, mine], cot),
    )):
        loads[k] = pltpu.make_async_copy(a, b, lsem.at[i])
        loads[k].start()

    barrier = pltpu.get_barrier_semaphore()
    pl.semaphore_signal(barrier, inc=1, device_id=peer, device_id_type=MESH)
    pl.semaphore_signal(barrier, inc=1, device_id=sib, device_id_type=MESH)
    for k in range(1, n):
        pl.semaphore_signal(barrier, inc=1, device_id=on_chip(k), device_id_type=MESH)

    sel = selector(hs)
    lane = lax.broadcasted_iota(jnp.int32, (PAD, 128), 1)
    sub = lax.broadcasted_iota(jnp.int32, (PAD, 128), 0)
    extra = jnp.where((sub == HEAD_DIM) | (sub == HEAD_DIM + 1), 1.0, 0.0)

    def head_weights(s):
        off = mm(sel, raw_offs[s], NT)
        for p in range(3):
            x = mm(sel, raw_proj[s, p]).astype(BF)
            for h in range(hs):
                a = s * srows + h * TRIPLE + p * PAD
                wt[a : a + PAD, :] = x[h * PAD : (h + 1) * PAD, :]
                if p != 1:
                    col = jnp.broadcast_to(off[h * PAD : (h + 1) * PAD, p // 2 : p // 2 + 1], (PAD, 128))
                    off_buf[a : a + PAD, :] = col + extra if p == 2 else col

    def project(s):
        def block(b, carry):
            t = pl.ds(pl.multiple_of(b * BT, BT), BT)
            x = mm(wt[s * srows : (s + 1) * srows, :], tok[:, t])
            for h in range(hs):
                for p in range(3):
                    a = s * srows + h * TRIPLE + p * PAD
                    y = x[h * TRIPLE + p * PAD : h * TRIPLE + (p + 1) * PAD, :]
                    if p != 1:
                        y = y + wide(off_buf[a : a + PAD, :])
                    if p == 0:
                        y = y * (SCALE * LOG2E)
                    qkv[a : a + PAD, t] = y.astype(BF)
            return carry

        lax.fori_loop(0, T // BT, block, 0)

    loads["proj"].wait()
    loads["offs"].wait()
    head_weights(0)
    loads["tok"].wait()
    project(0)

    pl.semaphore_wait(barrier, n + 1)
    fetched = ((proj_in, raw_proj, 0), (comb_in, raw_comb, 1), (up_in, raw_up, 1), (down_in, raw_down, 1))

    def fetch(i):
        a, b, _ = fetched[i]
        return remote(a, b.at[1], wsend.at[i, 0], wrecv.at[i], peer)

    def hand_on(i):
        b = fetched[i][1]
        return remote(b.at[1], b.at[1], wsend.at[i, 1], wrecv.at[i], sib)

    def only(c, todo, what):
        @pl.when(core == c)
        def _():
            for i in todo:
                what(i)

    def pass_on(i):
        fetch(i).wait()
        hand_on(i).start()

    bias_sends = [
        remote(thr_in, raw_thr.at[1], wsend.at[4, 0], wrecv.at[4], peer),
        remote(offs_in, raw_offs.at[1], wsend.at[5, 0], wrecv.at[5], peer),
    ]
    for cpy in bias_sends:
        cpy.start()
    only(0, (0,), lambda i: fetch(i).start())

    loads["rows"].wait()
    loads["cols"].wait()
    length = jnp.where(me == 0, len_in[0], len_in[1])
    for j in range(T // 128):
        q = slice(j * 128, (j + 1) * 128)
        live = lax.broadcasted_iota(jnp.int32, (128, 128), 0) + j * 128 < length
        thr_buf[q, :] = jnp.where(live, jnp.broadcast_to(rows[j : j + 1, :].astype(F32), (128, 128)).T, jnp.nan)
        vbuf[q, :] = jnp.broadcast_to(cols[j : j + 1, :].astype(F32), (128, 128)).T

    def visible(j, carry):
        q = pl.ds(pl.multiple_of(j * 128, 128), 128)
        rq = rows[pl.ds(j, 1), :].astype(F32)
        cq = cols[pl.ds(j, 1), :].astype(F32)
        rk = thr_buf[0:T, :]
        gap = rk * (rk - rq) * rq * (vbuf[0:T, :] - cq)
        bias[:, q] = jnp.where(gap == 0.0, 0.0, MASKED)
        return carry

    lax.fori_loop(0, T // 128, visible, 0)

    nq, KC = T // BT, 128

    def forward_head(h, carry):
        hq = pl.ds(pl.multiple_of(h * TRIPLE, PAD), PAD)
        hk = pl.ds(pl.multiple_of(h * TRIPLE + PAD, PAD), PAD)
        hv = pl.ds(pl.multiple_of(h * TRIPLE + 2 * PAD, PAD), PAD)
        peaks, kept = [None] * nq, {}
        k_buf[...] = qkv[hk, :].T

        def score(j, c):
            q, rr = slice(j * BT, (j + 1) * BT), slice(c * KC, (c + 1) * KC)
            s = mm(k_buf[rr, :], qkv[hq, q]) + bias[rr, q]
            kept[j, c] = s
            m = jnp.max(s.reshape(KC // 8, 8, BT), 0)
            peaks[j] = m if c == 0 else jnp.maximum(peaks[j], m)

        def expo(j, c):
            q, rr = slice(j * BT, (j + 1) * BT), slice(c * KC, (c + 1) * KC)
            if c == 0:
                peaks[j] = jnp.max(peaks[j], 0, keepdims=True)
            probs[h, rr, q] = jnp.exp2(kept.pop((j, c)) - peaks[j]).astype(BF)

        for j in range(nq + 1):
            for c in range(T // KC):
                if j < nq:
                    score(j, c)
                if j > 0:
                    expo(j - 1, c)
        o = mm(qkv[hv, :], probs[h])
        i = 1.0 / o[HEAD_DIM : HEAD_DIM + 1, :]
        inv[h] = i
        o = o * i
        ctx32[h] = o
        ctx[pl.ds(pl.multiple_of(h * PAD, PAD), PAD), :] = o.astype(BF)

        @pl.when(h == 1)
        def _():
            only(1, (1, 2, 3), lambda i: fetch(i).start())

        @pl.when(h == hs // 2)
        def _():
            only(0, (0,), pass_on)

        @pl.when(h == hs - 1)
        def _():
            only(0, (0,), lambda i: hand_on(i).wait_send())
            only(1, (0,), lambda i: hand_on(i).wait_recv())
            bias_sends[1].wait()
            head_weights(1)
            project(1)

        @pl.when(h == heads - 2)
        def _():
            only(1, (1, 2, 3), pass_on)

        return carry

    lax.fori_loop(0, heads, forward_head, 0)

    for k in ("comb", "up", "down", "thr", "corr", "gain", "shift", "cot"):
        loads[k].wait()
    only(1, (1, 2, 3), lambda i: hand_on(i).wait_send())
    only(0, (1, 2, 3), lambda i: hand_on(i).wait_recv())
    bias_sends[0].wait()

    def columns(x):
        k = x.shape[1]
        return jnp.broadcast_to(jnp.pad(x.astype(F32), ((0, 0), (0, up_to(k, 128) - k))), (128, up_to(k, 128))).T

    for s in range(2):
        cp[s * width : (s + 1) * width, :] = mm(sel, raw_comb[s]).astype(BF)
        upt[s * hst : s * hst + hid, :] = raw_up[s].T
        downn[s * hst : s * hst + hid, :] = raw_down[s].T
        upt[s * hst + hid : (s + 1) * hst, :] = jnp.zeros((hst - hid, D), BF)
        downn[s * hst + hid : (s + 1) * hst, :] = jnp.zeros((hst - hid, D), BF)
        thr_buf[s * hst : (s + 1) * hst, :] = columns(raw_thr[s])[0:hst, :]
    cpt[...] = cp[...].T
    for i in range(6):
        x = (raw_corr, raw_gain, raw_shift)[i // 2][...].astype(F32)
        vbuf[i * D : (i + 1) * D, :] = columns(x[i % 2 : i % 2 + 1, :])[0:D, :]
    one_row = jnp.where(lax.broadcasted_iota(jnp.int32, (8, T), 0) == 0, 1.0, 0.0).astype(BF)
    first_low[D : D + 8, :] = one_row
    acc[...] = jnp.zeros_like(acc)

    def vec(i):
        return wide(vbuf[i * D : (i + 1) * D, :])

    def norm(x):
        x = x - jnp.mean(x, 0, keepdims=True)
        rs = lax.rsqrt(jnp.mean(x * x, 0, keepdims=True) + EPS)
        return x * rs, rs

    def norm_back(dy, xhat, rs, g):
        d = dy * g
        return rs * (d - jnp.mean(d, 0, keepdims=True) - xhat * jnp.mean(d * xhat, 0, keepdims=True))

    lanes = lax.broadcasted_iota(jnp.int32, (D, 128), 1)

    def tally(i, v):
        acc[...] += jnp.where(lanes == i, jnp.sum(v, 1, keepdims=True), 0.0)

    HC = hst // 2

    def send_out(b):
        t = pl.ds(pl.multiple_of(b * BT, BT), BT)
        there = pl.ds(pl.multiple_of(me * T + b * BT, BT), BT)
        return remote(cot.at[:, t], lo_out.at[:, there], osend.at[b], orecv.at[b], peer)

    def middle(b, carry):
        t = pl.ds(pl.multiple_of(b * BT, BT), BT)
        att = mm(cpt[...], ctx[:, t])
        x1, rs1 = norm(tok[:, t].astype(F32) + att + vec(0))
        first = x1 * vec(2) + vec(4)
        low = first.astype(BF)
        first_low[0:D, t] = low
        for j in range(4):
            u = slice(j * HC, (j + 1) * HC)
            pre = mm(upt[u, :], low) + wide(thr_buf[u, :])
            cdf, pdf = phi_pair(pre)
            act[u, t] = (pre * cdf).astype(BF)
            dpre[u, t] = (cdf + pre * pdf).astype(BF)
        dn = mm(raw_down[0], act[0:hid, t]) + mm(raw_down[1], act[hst : hst + hid, t])
        x2, rs2 = norm(first + dn + vec(1))
        dy = cot[:, t].astype(F32)
        cot[:, t] = (x2 * vec(3) + vec(5)).astype(BF)
        send_out(b).start()
        tally(0, dy * x2)
        tally(1, dy)
        dr2 = norm_back(dy, x2, rs2, vec(3))
        tally(2, dr2)
        dd = dr2.astype(BF)
        d_down[:, t] = dd
        for j in range(4):
            u = slice(j * HC, (j + 1) * HC)
            dpre[u, t] = (mm(downn[u, :], dd) * dpre[u, t].astype(F32)).astype(BF)
        df = dr2 + mm(raw_up[0], dpre[0:hid, t]) + mm(raw_up[1], dpre[hst : hst + hid, t])
        tally(3, df * x1)
        tally(4, df)
        dr1 = norm_back(df, x1, rs1, vec(2))
        tally(5, dr1)
        bias[0:D, t] = dr1
        da = dr1.astype(BF)
        d_att[:, t] = da
        dctx[:, t] = mm(cp[...], da).astype(BF)
        return carry

    lax.fori_loop(0, T // BT, middle, 0)

    def all_of(ref, sem):
        pltpu.make_async_copy(ref, ref, sem).wait()

    def step(g, k):
        buf, half, quarter, gat = r[f"buf{g}"], r[f"half{g}"], r[f"quarter{g}"], r[f"gat{g}"]
        sizes, swap = plan.levels[g]
        rows_at = plan.blocks(g)
        top = len(sizes)
        strides = [1]
        for z in sizes:
            strides.append(strides[-1] * z)
        digit = [lax.rem(lax.div(chip, strides[j]), sizes[j]) for j in range(top)]
        spread = top - 1 if swap else top

        def member(j, i):
            d = lax.rem(digit[j] + i, sizes[j])
            return {"dp": (chip + (d - digit[j]) * strides[j]) * 2 + core}, d

        def held(j):
            return buf.at[core, 0] if j == 0 else r[f"sum{g}_{j - 1}"]

        def place(j):
            o = 0
            for i in range(j + 1):
                o = o + digit[i] * rows_at[i + 1]
            return pl.ds(pl.multiple_of(o, 16), rows_at[j + 1])

        def land(j):
            return r[f"land{g}_{j}"]

        def total(j):
            m = rows_at[j + 1]
            if j < spread:
                t = held(j)[pl.ds(pl.multiple_of(digit[j] * m, 16), m), :].astype(F32)
            else:
                t = held(j)[...].astype(F32)
            for i in range(sizes[j] - 1):
                t = t + land(j)[i].astype(F32)
            r[f"sum{g}_{j}"][...] = t.astype(BF)

        c1 = lambda: remote(buf.at[1 - core], half, gsend.at[g, 0], grecv.at[g, 0], sib)
        c2 = lambda: remote(buf.at[core, 1], quarter, gsend.at[g, 1], grecv.at[g, 1], peer)
        cl = lambda: remote(gat.at[core], gat.at[core], gsend.at[g, 2], grecv.at[g, 2], sib)
        own = lambda: pltpu.make_async_copy(r[f"sum{g}_{top - 1}"], gat.at[core, place(spread - 1), :], gloc.at[g])
        down_sem, up_sem = 3, 3 + top

        if k == 2:
            c1().wait()
            buf[core] = (buf[core].astype(F32) + half[...].astype(F32)).astype(BF)
        if k == 3:
            c2().wait()
            buf[core, 0] = (buf[core, 0].astype(F32) + quarter[...].astype(F32)).astype(BF)
        if 4 <= k < 4 + top:
            j = k - 4
            all_of(land(j), gsend.at[g, down_sem + j])
            all_of(land(j), grecv.at[g, down_sem + j])
            total(j)
        up = k - 3 - top
        if 1 <= up <= spread:
            j = spread - up
            if up == 1:
                own().wait()
            for sem in (gsend, grecv):
                part = gat.at[core, 0 : (sizes[j] - 1) * rows_at[j + 1], :]
                pltpu.make_async_copy(part, part, sem.at[g, up_sem + j]).wait()
        if k == 4 + top + spread:
            cl().wait()
            result(g).start()

        if k == 1:
            c1().start()
        if k == 2:
            c2().start()
        if 3 <= k < 3 + top:
            j = k - 3
            m = rows_at[j + 1]
            for i in range(1, sizes[j]):
                dev, d = member(j, i)
                src = held(j).at[pl.ds(pl.multiple_of(d * m, 16), m), :] if j < spread else held(j)
                remote(src, land(j).at[i - 1], gsend.at[g, down_sem + j], grecv.at[g, down_sem + j], dev).start()
        if 0 <= up < spread:
            j = spread - 1 - up
            if up == 0:
                own().start()
            for i in range(1, sizes[j]):
                dev, _ = member(j, i)
                src = r[f"sum{g}_{top - 1}"] if up == 0 else gat.at[core, place(j), :]
                remote(src, gat.at[core, place(j), :], gsend.at[g, up_sem + j], grecv.at[g, up_sem + j], dev).start()
        if k == 3 + top + spread:
            cl().start()

    def result(g):
        return pltpu.make_async_copy(r[f"gat{g}"], r[f"gat_out{g}"], gloc.at[g])

    def steps(g):
        sizes, swap = plan.levels[g]
        return 4 + 2 * len(sizes) - (1 if swap else 0)

    def put(g, s, base, x):
        buf = r[f"buf{g}"]
        hr = x.shape[0] // 2
        x = x.astype(BF)
        for l in range(up_to(x.shape[1], 128) // 128):
            wl = min(128, x.shape[1] - l * 128)
            for c in range(2):
                a = base + l * hr
                y = x[c * hr : (c + 1) * hr, l * 128 : l * 128 + wl]
                if wl == 64:
                    buf[c, s, a : a + hr // 2, :] = jnp.concatenate([y[: hr // 2], y[hr // 2 :]], 1)
                else:
                    buf[c, s, a : a + hr, 0:wl] = y

    def clear(g, rows_used):
        buf = r[f"buf{g}"]
        if rows_used < buf.shape[2]:
            buf[:, :, rows_used:, :] = jnp.zeros((2, 2, buf.shape[2] - rows_used, 128), BF)

    (gd, bd), (gu, bu), (gc, bc), (gs, bs) = plan.down, plan.up, plan.comb, plan.small
    for s in range(2):
        u = slice(s * hst, (s + 1) * hst)
        x = mm(d_down[...], act[u, :], NT)
        put(gd, s, bd, jnp.concatenate([x, jnp.zeros((8, hst), F32)], 0))
    clear(gd, plan.used[gd])
    step(gd, 1)
    sums = acc[...].T[0:8, :]
    hi = sums.astype(BF).astype(F32)
    for s in range(2):
        u = slice(s * hst, (s + 1) * hst)
        put(gu, s, bu, mm(first_low[...], dpre[u, :], NT))
        x = mm(ctx[s * width : (s + 1) * width, :], d_att[...], NT)
        put(gc, s, bc, jnp.concatenate([x, jnp.zeros((width, 8), F32)], 1))
        for l in range(3):
            wl = min(128, D - l * 128)
            x = jnp.concatenate([hi, sums - hi], 0)[:, l * 128 : l * 128 + wl].astype(BF)
            for c in range(2):
                r[f"buf{gs}"][c, s, bs + l * 16 : bs + (l + 1) * 16, 0:wl] = x
    clear(gu, plan.used[gu])
    step(gu, 1)
    first_low[0:D, :] = tok[...]

    lo_here = pltpu.make_async_copy(cot, lo_out.at[:, mine], lsem.at[13])
    lo_here.start()

    def part_grads(i):
        first, g = sum(plan.parts[:i]), plan.first_part + i
        for s in range(2):
            a = s * srows + first * TRIPLE
            put(g, s, 0, mm(dxt[a : a + plan.parts[i] * TRIPLE, :], first_low[...], NT))
        clear(g, plan.used[g])

    last = len(plan.rows) - 1

    def backward_head(i, carry):
        h = lax.rem(i, 2) * hs + lax.div(i, 2)
        hq = pl.ds(pl.multiple_of(h * TRIPLE, PAD), PAD)
        hk = pl.ds(pl.multiple_of(h * TRIPLE + PAD, PAD), PAD)
        hv = pl.ds(pl.multiple_of(h * TRIPLE + 2 * PAD, PAD), PAD)
        rowi = lax.broadcasted_iota(jnp.int32, (PAD, T), 0)
        scaled = (dctx[pl.ds(pl.multiple_of(h * PAD, PAD), PAD), :].astype(F32) * inv[h]).astype(BF).astype(F32)
        nd = -jnp.sum(scaled * ctx32[h], 0, keepdims=True)
        nh = nd.astype(BF).astype(F32)
        da = jnp.where(rowi == HEAD_DIM, nh, jnp.where(rowi == HEAD_DIM + 1, nd - nh, scaled)).astype(BF)
        k_buf[...] = qkv[hv, :].T
        qt, kt = qkv[hq, :], qkv[hk, :]
        dq = jnp.zeros((PAD, T), F32)
        for j in range(T // BT):
            rr = slice(j * BT, (j + 1) * BT)
            pk = probs[h, rr, :]
            dxt[hv, rr] = mm(da, pk, NT).astype(BF)
            ds = (pk.astype(F32) * mm(k_buf[rr, :], da)).astype(BF)
            dxt[hk, rr] = (mm(qt, ds, NT) * (1.0 / LOG2E)).astype(BF)
            dq = dq + mm(kt[:, rr], ds)
        dxt[hq, :] = (dq * SCALE).astype(BF)

        for at, todo in plan.schedule.items():
            @pl.when(i == at)
            def _(todo=todo):
                for what in todo:
                    if what == "part0":
                        part_grads(0)
                    else:
                        step(*what)
        return carry

    lax.fori_loop(0, heads, backward_head, 0)

    part_grads(len(plan.parts) - 1)
    w_rows = up_to(D, 16)

    def turn_weights():
        for a in range(0, 2 * srows, T):
            b = min(T, 2 * srows - a)
            o = a // T * w_rows
            dpre[o : o + D, 0:b] = wt[a : a + b, :].T

    def input_block(b):
        t = slice(b * BT, (b + 1) * BT)
        x = bias[0:D, t]
        for a in range(0, 2 * srows, T):
            e = min(T, 2 * srows - a)
            o = a // T * w_rows
            x = x + mm(dpre[o : o + D, 0:e], dxt[a : a + e, t])
        bias[0:D, t] = x
        d_down[:, t] = x.astype(BF)

    def move(b):
        t = slice(b * BT, (b + 1) * BT)
        return remote(d_down.at[:, t], dxp_out.at[:, t], xsend.at[b], xrecv.at[b], peer)

    dx_here = pltpu.make_async_copy(bias.at[0:D, :], dxo_out, lsem.at[14])
    done, sent = 0, None
    for what in plan.after:
        if what == "w":
            turn_weights()
        elif what == "send":
            sent = 0
        elif isinstance(what, int):
            input_block(what)
            done += 1
            if done == T // BT:
                dx_here.start()
        else:
            step(*what)
        while sent is not None and sent < done:
            move(sent).start()
            sent += 1
    for g in range(last + 1):
        result(g).wait()
    lo_here.wait()
    for b in range(T // BT):
        send_out(b).wait()
    dx_here.wait()
    for b in range(T // BT):
        move(b).wait()


def final_kernel(hs, plan, lo_in, dxo_in, dxp_in, *refs):
    ng = len(plan.rows)
    gat_in = refs[:ng]
    lo, dx, proj, off, comb, exp, thr, con, corr, gains, shifts, xp, xc, half, peer_half, own_half, lo_buf, sems, *gats = refs[ng:]
    D, T = dxp_in.shape
    me = lax.axis_index("tensor")
    own = pl.ds(pl.multiple_of(me * T, T), T)
    other = pl.ds(pl.multiple_of((1 - me) * T, T), T)
    fetch = [pltpu.make_async_copy(dxp_in, peer_half, sems.at[3]), pltpu.make_async_copy(dxo_in, own_half, sems.at[4]), pltpu.make_async_copy(lo_in, lo_buf, sems.at[5])]
    fetch += [pltpu.make_async_copy(a, b, sems.at[6 + i]) for i, (a, b) in enumerate(zip(gat_in, gats))]
    for c in fetch:
        c.start()
    copies = [
        pltpu.make_async_copy(half, dx.at[:, other], sems.at[0]), pltpu.make_async_copy(own_half, dx.at[:, own], sems.at[1]), pltpu.make_async_copy(lo_buf, lo, sems.at[2]),
    ]
    fetch[0].wait()
    half[...] = peer_half[...].astype(F32)
    copies[0].start()
    for i in (1, 2):
        fetch[i].wait()
        copies[i].start()
    for c in fetch[3:]:
        c.wait()

    (gd, bd), (gu, bu), (gc, bc), (gs, bs) = plan.down, plan.up, plan.comb, plan.small
    hid = exp.shape[1]
    width = hs * PAD
    sel = selector(hs)
    for c in range(2):
        for l in range(5):
            wl = min(128, hid - l * 128)
            ls = slice(l * 128, l * 128 + wl)
            rows = min(160, D - c * 160)
            con[c * 160 : c * 160 + rows, ls] = gats[gd][c, bd + l * 160 : bd + l * 160 + rows, 0:wl].astype(F32)
            exp[c * 160 : c * 160 + rows, ls] = gats[gu][c, bu + l * 160 : bu + l * 160 + rows, 0:wl].astype(F32)
            if c == 1:
                x = gats[gu][c, bu + l * 160 + 144 : bu + l * 160 + 160, 0:wl].astype(F32)
                thr[0:1, ls] = x[D - 160 - 144 : D - 160 - 143, :]

    def unfold(g, c, base, hr, l):
        a = base + l * hr
        if l < 2:
            return gats[g][c, a : a + hr, :]
        x = gats[g][c, a : a + hr // 2, :]
        return jnp.concatenate([x[:, 0:64], x[:, 64:128]], 0)

    for c in range(2):
        hr = width // 2
        for l in range(3):
            x = unfold(gc, c, bc, hr, l)
            xc[c * hr : (c + 1) * hr, l * 128 : l * 128 + x.shape[1]] = x
    comb[...] = mm(sel, xc[:, 0:D], TN)
    for l in range(3):
        wl = min(128, D - l * 128)
        ls = slice(l * 128, l * 128 + wl)
        a = bs + l * 16
        x = gats[gs][0, a : a + 16, 0:wl].astype(F32)
        x = x[0:8, :] + x[8:16, :]
        gains[1:2, ls] = x[0:1, :]
        shifts[1:2, ls] = x[1:2, :]
        corr[1:2, ls] = x[2:3, :]
        gains[0:1, ls] = x[3:4, :]
        shifts[0:1, ls] = x[4:5, :]
        corr[0:1, ls] = x[5:6, :]
    first = 0
    for i, hp in enumerate(plan.parts):
        hr = hp * TRIPLE // 2
        for c in range(2):
            for l in range(3):
                x = unfold(plan.first_part + i, c, 0, hr, l)
                for u in range(hr // 16):
                    v = c * (hr // 16) + u
                    h, p, q = first + v // 6, v % 6 // 2, v % 2
                    a = h * PAD + q * 16
                    xp[p, a : a + 16, l * 128 : l * 128 + x.shape[1]] = x[u * 16 : (u + 1) * 16, :]
        first += hp
    for p in range(3):
        proj[p] = mm(sel, xp[p, :, 0:D], TN)
    for i, p in ((0, 0), (1, 2)):
        t = mm(xp[p, :, 256:320], sel, TN)
        off[i : i + 1, :] = t[D - 256 : D - 255, :]
    for c in copies:
        c.wait()


def shards(n, tokens, projection, offsets, combiner, expansion, thresholds, contraction, corrections, gains, shifts, table_rows, table_columns, table_lengths, cotangent):
    tables = table_lengths.shape[0]
    T, D = tokens.shape[0] // tables, tokens.shape[1]
    part, hid = projection.shape[2], thresholds.shape[0]
    hs = part // HEAD_DIM
    W = hs * PAD
    R = hs * TRIPLE
    hst = up_to(hid, 16)

    ins = (
        tokens.T, cotangent.T, projection.transpose(0, 2, 1), combiner, expansion, contraction.T, thresholds.reshape(1, hid), offsets, corrections, gains, shifts,
        table_rows.reshape(-1, 128), table_columns.reshape(-1, 128), table_lengths,
    )
    plan = Plan(n, hs)
    H = plan.rows
    G = len(H)
    outs = [((D, tables * T), BF), ((D, T), F32), ((D, T), BF)] + [((2, h, 128), BF) for h in H]
    out_names = ["lo_out", "dxo_out", "dxp_out"] + [f"gat_out{g}" for g in range(G)]
    V = pltpu.VMEM
    sem = pltpu.SemaphoreType.DMA
    scratch = {
        "tok": V((D, T), BF), "cot": V((D, T), BF), "first_low": V((D + 8, T), BF), "d_down": V((D, T), BF), "d_att": V((D, T), BF),
        "raw_proj": V((2, 3, part, D), BF), "raw_comb": V((2, part, D), BF), "raw_up": V((2, D, hid), BF), "raw_down": V((2, D, hid), BF), "raw_thr": V((2, 1, hid), BF), "raw_offs": V((2, 2, part), BF), "raw_corr": V((2, D), BF), "raw_gain": V((2, D), BF), "raw_shift": V((2, D), BF),
        "wt": V((2 * R, D), BF), "cp": V((2 * W, D), BF), "cpt": V((D, 2 * W), BF), "upt": V((2 * hst, D), BF), "downn": V((2 * hst, D), BF),
        "qkv": V((2 * R, T), BF), "bias": V((T, T), F32), "probs": V((2 * hs, T, T), BF), "ctx32": V((2 * hs, PAD, T), F32), "ctx": V((2 * W, T), BF),
        "inv": V((2 * hs, 1, T), F32), "dctx": V((2 * W, T), BF), "dxt": V((max(2 * R, 2 * hst), T), BF), "dpre": V((2 * hst, T), BF),
        "vbuf": V((6 * D, 128), F32), "thr_buf": V((2 * hst, 128), F32), "off_buf": V((2 * R, 128), F32), "acc": V((D, 128), F32), "k_buf": V((T, PAD), BF),
        "rows": V((T // 128, 128), jnp.int32), "cols": V((T // 128, 128), jnp.int32),
        "lsem": sem((15,)), "wsend": sem((6, 2)), "wrecv": sem((6,)), "gsend": sem((G, 9)), "grecv": sem((G, 9)), "gloc": sem((G,)),
        "osend": sem((T // BT,)), "orecv": sem((T // BT,)), "xsend": sem((T // BT,)), "xrecv": sem((T // BT,)),
    }
    for g, h in enumerate(H):
        scratch[f"buf{g}"] = V((2, 2, h, 128), BF)
        scratch[f"half{g}"] = V((2, h, 128), BF)
        scratch[f"gat{g}"] = V((2, h, 128), BF)
        scratch[f"quarter{g}"] = V((h, 128), BF)
        sizes, _ = plan.levels[g]
        for j, z in enumerate(sizes):
            scratch[f"land{g}_{j}"] = V((z - 1, plan.blocks(g)[j + 1], 128), BF)
            scratch[f"sum{g}_{j}"] = V((plan.blocks(g)[j + 1], 128), BF)
    anywhere = pl.BlockSpec(memory_space=pl.ANY)
    vmem = pl.BlockSpec(memory_space=pltpu.VMEM)
    lo, dxo, dxp, *gats = pl.pallas_call(
        functools.partial(main_kernel, n, hs, plan, list(INPUTS) + out_names + list(scratch)),
        out_shape=[jax.ShapeDtypeStruct(s, d) for s, d in outs],
        in_specs=[anywhere] * (len(ins) - 1) + [pl.BlockSpec(memory_space=pltpu.SMEM)],
        out_specs=[anywhere] * len(outs),
        scratch_shapes=list(scratch.values()),
        compiler_params=pltpu.CompilerParams(vmem_limit_bytes=63 * 2 ** 20, collective_id=0, has_side_effects=True),
    )(*ins)
    finals = [
        ((D, tables * T), BF), ((D, tables * T), F32), ((3, part, D), F32), ((2, part), F32), ((part, D), F32), ((D, hid), F32),
        ((1, hid), F32), ((D, hid), F32), ((2, D), F32), ((2, D), F32), ((2, D), F32),
    ]
    lo, dx, proj, off, comb, exp, thr, con, corr, gn, sh = pl.pallas_call(
        functools.partial(final_kernel, hs, plan),
        out_shape=[jax.ShapeDtypeStruct(s, d) for s, d in finals],
        in_specs=[pl.BlockSpec(memory_space=pltpu.HBM)] * (3 + G),
        out_specs=[anywhere, anywhere] + [vmem] * 9,
        scratch_shapes=[V((3, W, 384), BF), V((W, 384), BF), V((D, T), F32), V((D, T), BF), V((D, T), F32), V((D, tables * T), BF), sem((6 + G,))] + [V((2, h, 128), BF) for h in H],
        compiler_params=pltpu.CompilerParams(vmem_limit_bytes=62 * 2 ** 20),
    )(lo, dxo, dxp, *gats)
    return lo.T, dx.T, proj.transpose(0, 2, 1), off, comb, exp, thr.reshape(hid), con.T, corr, gn, sh


def solution(mesh):
    return jax.shard_map(
        functools.partial(shards, mesh.shape["dp"] // 2),
        mesh=mesh,
        in_specs=(
            P("dp", None), P(None, None, "tensor"), P(None, "tensor"), P("tensor", None), P(None, "tensor"), P("tensor"),
            P("tensor", None), P(), P(), P(), P("dp"), P("dp"), P("dp"), P("dp", None),
        ),
        out_specs=(
            P("dp", None), P("dp", None), P(None, None, "tensor"), P(None, "tensor"), P("tensor", None), P(None, "tensor"),
            P("tensor"), P("tensor", None), P(), P(), P(),
        ),
        check_vma=False,
    )
```

time: 300 us -> 112 us (0.37)
  waiting for transfers between devices: 76.5 us -> 0 us
  blocking collectives: 49.1 us -> 0 us
  local copies, waits for them, and re-layouts: 40.3 us -> 1.26 us
  Pallas kernels: 85.2 us -> 109 us
  other arithmetic: 19.5 us -> 1.29 us
  starting transfers between devices: 13.8 us -> 0 us
  between operations: 14.3 us -> 0.66 us
    psum x1 -> x0, blocking collectives: 49.1 us -> none  [shards(): small = lax.psum(small, ('dp', 'tensor'))[:, :D]]
    ppermute x12 -> x0, waiting for transfers between devices: 41.3 us -> none  [other(): return lax.ppermute(x, 'tensor', swap)]
    psum x1 -> x0, waiting for transfers between devices: 35.2 us -> none  [reduced(): return lax.psum(x[0].astype(F32) + other(x[1].astype(BF)).astype(F32), 'dp')]
    pallas_call x1 -> x2, Pallas kernels: 85.2 us -> 109 us  [the longest x1 104 us: shards(): pl.pallas_call(functools.partial(main_kernel, n, hs, plan, list(INPUTS) +...]
    ppermute x12 -> x0, starting transfers between devices: 13.8 us -> none  [other(): return lax.ppermute(x, 'tensor', swap)]
    unnamed x33 -> x0, local copies, waits for them, and re-layouts: 10.7 us -> none
    another operation x9 -> x0, other arithmetic: 9.72 us -> none  [the longest x5 7.38 us: pair(): return jnp.stack((x, other(x)))]
    reshape x6 -> x1, local copies, waits for them, and re-layouts: 7.92 us -> 1.26 us  [shards(): thresholds.reshape(1, hid)]
  transfers between devices with their start and end apart: 13 -> 0, of which waited for: 5 -> 0; matrix products, arithmetic and copies ran while one was open for 15% -> 0% of each run, Pallas kernels for 0% -> 0%
where the time goes in v2:
time: 112 us
  Pallas kernels  109 us (97%)
  other arithmetic  1.29 us (1%)
  local copies, waits for them, and re-layouts  1.26 us (1%)
    pallas_call x1, Pallas kernels, shards(): pl.pallas_call(functools.partial(main_kernel, n, hs, plan, list(INPUTS) +...  104 us
    pallas_call x1, Pallas kernels, shards(): pl.pallas_call(functools.partial(final_kernel, hs, plan), out_shape=[jax....  4.82 us

profile of v2, /device:TPU:0, one launch (start us, length us, event | category | flops | bytes accessed | tf_op | source)
XLA Modules:
  0.0 111.7 jit_solution(7855734608041206470)
XLA Ops:
  0.6 1.3 %reshape.34.refs_6_ = bf16[1,600]{1,0:T(2,128)(2,1)} reshape(bf16[600]{0:T(1024)(128)(2,1)} %param.19) | data formatting | bytes 2400 | tf_op jit(solution)/shard_map/reshape | solution.py:716
  1.9 103.7 %shard_map.221 = (bf16[312,2048]{1,0:T(8,128)(2,1)}, f32[312,1024]{1,0:T(8,128)}, bf16[312,1024]{1,0:T(8,128)(2,1)}, bf16[2,832,128]{2,1,0:T(8,128)(2,1)}, bf16[...) custom-call(bf16[312,2048]{1,0:T(8,128)(2,1)} %bitcast.10, ...), custom_call_target="tpu_custom_call" | custom-call | tf_op jit(solution)/shard_map/pallas_call | solution.py:748
  105.6 4.8 %shard_map.222 = (bf16[312,2048]{1,0:T(8,128)(2,1)}, f32[312,2048]{1,0:T(8,128)}, f32[3,156,312]{2,1,0:T(8,128)}, f32[2,156]{1,0:T(2,128)}, f32[156,312]{1,0:T(8...) custom-call(bf16[312,2048]{1,0:T(8,128)(2,1)} %get-tuple-element.29., ...), custom_call_target="tpu_custom_call" | custom-call | tf_op jit(solution)/shard_map/pallas_call | solution.py:760
  110.4 1.3 %reduce = f32[600]{0:T(1024)} reduce(f32[1,600]{1,0:T(1,128)} %get-tuple-element.42, f32[]{:T(128)} %constant.1), dimensions={0}, to_apply=%get-tuple-element.42.reduce_sub_computation | reduce | bytes 4804 | tf_op jit(solution)/shard_map/pallas_call | solution.py:760

commit v3 on v2

--- a/solution.py
+++ b/solution.py
@@ -86,9 +86,10 @@
 
 
 PARTS = (4, 2)
+LAG, STAGES, EARLY = 1, 15, 2
 FLAT = (False, False, False, True)
-SCHEDULE = {0: [(0, 2)], 1: [(1, 2)], 3: [(0, 3)], 5: [(0, 4), (1, 3)], 7: ["part0", (2, 1), (0, 5), (1, 4)], 8: [(2, 2)], 9: [(0, 6), (1, 5)], 10: [(2, 3), (0, 7)], 11: [(1, 6), (2, 4)]}
-AFTER = [(3, 1), "w", 0, (3, 2), "send", 1, (1, 7), (2, 5), 2, (3, 3), 3, (2, 6), (3, 4), (2, 7), (3, 5), (3, 6)]
+SCHEDULE = {0: [(1, 2)], 2: [(0, 3)], 3: ["lo", "part0", (2, 1), (0, 4), (1, 3)], 4: [(2, 2), (0, 5)], 5: [(0, 6), (1, 4)]}
+AFTER = [(3, 1), 0, (3, 2), "send", 1, (2, 3), (0, 7), (1, 5), 2, 3, (3, 3), (2, 4), (1, 6), (3, 4), (2, 5), (1, 7), (2, 6), (3, 5), (2, 7), (3, 6)]
 
 
 def main_kernel(n, hs, plan, names, *refs):
@@ -102,7 +103,7 @@
     qkv, bias, probs, ctx32, ctx, inv, dctx, dxt, dpre = (
         r[k] for k in ("qkv", "bias", "probs", "ctx32", "ctx", "inv", "dctx", "dxt", "dpre")
     )
-    vbuf, thr_buf, off_buf, acc, k_buf = (r[k] for k in ("vbuf", "thr_buf", "off_buf", "acc", "k_buf"))
+    thr_buf, acc, k_buf, da_buf = (r[k] for k in ("thr_buf", "acc", "k_buf", "da_buf"))
     rows, cols, lsem, wsend, wrecv, gsend, grecv, gloc, osend, orecv, xsend, xrecv = (
         r[k] for k in ("rows", "cols", "lsem", "wsend", "wrecv", "gsend", "grecv", "gloc", "osend", "orecv", "xsend", "xrecv")
     )
@@ -160,7 +161,7 @@
                 wt[a : a + PAD, :] = x[h * PAD : (h + 1) * PAD, :]
                 if p != 1:
                     col = jnp.broadcast_to(off[h * PAD : (h + 1) * PAD, p // 2 : p // 2 + 1], (PAD, 128))
-                    off_buf[a : a + PAD, :] = col + extra if p == 2 else col
+                    thr_buf[a : a + PAD, :] = col + extra if p == 2 else col
 
     def project(s):
         def block(b, carry):
@@ -171,7 +172,7 @@
                     a = s * srows + h * TRIPLE + p * PAD
                     y = x[h * TRIPLE + p * PAD : h * TRIPLE + (p + 1) * PAD, :]
                     if p != 1:
-                        y = y + wide(off_buf[a : a + PAD, :])
+                        y = y + wide(thr_buf[a : a + PAD, :])
                     if p == 0:
                         y = y * (SCALE * LOG2E)
                     qkv[a : a + PAD, t] = y.astype(BF)
@@ -221,14 +222,14 @@
         q = slice(j * 128, (j + 1) * 128)
         live = lax.broadcasted_iota(jnp.int32, (128, 128), 0) + j * 128 < length
         thr_buf[q, :] = jnp.where(live, jnp.broadcast_to(rows[j : j + 1, :].astype(F32), (128, 128)).T, jnp.nan)
-        vbuf[q, :] = jnp.broadcast_to(cols[j : j + 1, :].astype(F32), (128, 128)).T
+        dxt[q, 0:128] = jnp.broadcast_to(cols[j : j + 1, :].astype(F32), (128, 128)).T.astype(BF)
 
     def visible(j, carry):
         q = pl.ds(pl.multiple_of(j * 128, 128), 128)
         rq = rows[pl.ds(j, 1), :].astype(F32)
         cq = cols[pl.ds(j, 1), :].astype(F32)
         rk = thr_buf[0:T, :]
-        gap = rk * (rk - rq) * rq * (vbuf[0:T, :] - cq)
+        gap = rk * (rk - rq) * rq * (dxt[0:T, 0:128].astype(F32) - cq)
         bias[:, q] = jnp.where(gap == 0.0, 0.0, MASKED)
         return carry
 
@@ -236,48 +237,51 @@
 
     nq, KC = T // BT, 128
 
-    def forward_head(h, carry):
-        hq = pl.ds(pl.multiple_of(h * TRIPLE, PAD), PAD)
-        hk = pl.ds(pl.multiple_of(h * TRIPLE + PAD, PAD), PAD)
-        hv = pl.ds(pl.multiple_of(h * TRIPLE + 2 * PAD, PAD), PAD)
-        peaks, kept = [None] * nq, {}
-        k_buf[...] = qkv[hk, :].T
-
-        def score(j, c):
-            q, rr = slice(j * BT, (j + 1) * BT), slice(c * KC, (c + 1) * KC)
-            s = mm(k_buf[rr, :], qkv[hq, q]) + bias[rr, q]
-            kept[j, c] = s
-            m = jnp.max(s.reshape(KC // 8, 8, BT), 0)
-            peaks[j] = m if c == 0 else jnp.maximum(peaks[j], m)
-
-        def expo(j, c):
-            q, rr = slice(j * BT, (j + 1) * BT), slice(c * KC, (c + 1) * KC)
-            if c == 0:
-                peaks[j] = jnp.max(peaks[j], 0, keepdims=True)
-            probs[h, rr, q] = jnp.exp2(kept.pop((j, c)) - peaks[j]).astype(BF)
-
-        for j in range(nq + 1):
+    def weigh(h, j):
+        q = slice(j * BT, (j + 1) * BT)
+        o = mm(qkv[pl.ds(pl.multiple_of(h * TRIPLE + 2 * PAD, PAD), PAD), :], probs[h, :, q])
+        i = 1.0 / o[HEAD_DIM : HEAD_DIM + 1, :]
+        inv[h, :, q] = i
+        o = o * i
+        ctx32[h, :, q] = o
+        ctx[pl.ds(pl.multiple_of(h * PAD, PAD), PAD), q] = o.astype(BF)
+
+    def forward_pair(i, carry):
+        before = lax.rem(2 * i + heads - 2, heads)
+        for e in range(2):
+            k_buf[e] = qkv[pl.ds(pl.multiple_of((2 * i + e) * TRIPLE + PAD, PAD), PAD), :].T
+        last_block = None
+        for u in range(2 * nq + 1):
+            if u < 2 * nq:
+                e, j = divmod(u, nq)
+                q = slice(j * BT, (j + 1) * BT)
+                hq = pl.ds(pl.multiple_of((2 * i + e) * TRIPLE, PAD), PAD)
+                scores, peak = [], None
+            if last_block is not None:
+                ph, pq, ps, pm = last_block
+                pm = jnp.max(pm, 0, keepdims=True)
             for c in range(T // KC):
-                if j < nq:
-                    score(j, c)
-                if j > 0:
-                    expo(j - 1, c)
-        o = mm(qkv[hv, :], probs[h])
-        i = 1.0 / o[HEAD_DIM : HEAD_DIM + 1, :]
-        inv[h] = i
-        o = o * i
-        ctx32[h] = o
-        ctx[pl.ds(pl.multiple_of(h * PAD, PAD), PAD), :] = o.astype(BF)
-
-        @pl.when(h == 1)
+                rr = slice(c * KC, (c + 1) * KC)
+                if u < 2 * nq:
+                    x = mm(k_buf[e, rr, :], qkv[hq, q]) + bias[rr, q]
+                    scores.append(x)
+                    m = jnp.max(x.reshape(KC // 8, 8, BT), 0)
+                    peak = m if c == 0 else jnp.maximum(peak, m)
+                if last_block is not None:
+                    probs[ph, rr, pq] = jnp.exp2(ps[c] - pm).astype(BF)
+            if u < 2 * nq:
+                weigh(before + e, j)
+                last_block = (2 * i + e, q, scores, peak)
+
+        @pl.when(i == 0)
         def _():
             only(1, (1, 2, 3), lambda i: fetch(i).start())
 
-        @pl.when(h == hs // 2)
+        @pl.when(i == hs // 4)
         def _():
             only(0, (0,), pass_on)
 
-        @pl.when(h == hs - 1)
+        @pl.when(i == hs // 2 - 1)
         def _():
             only(0, (0,), lambda i: hand_on(i).wait_send())
             only(1, (0,), lambda i: hand_on(i).wait_recv())
@@ -285,13 +289,16 @@
             head_weights(1)
             project(1)
 
-        @pl.when(h == heads - 2)
+        @pl.when(i == hs - 2)
         def _():
             only(1, (1, 2, 3), pass_on)
 
         return carry
 
-    lax.fori_loop(0, heads, forward_head, 0)
+    lax.fori_loop(0, hs, forward_pair, 0)
+    for e in range(2):
+        for j in range(nq):
+            weigh(heads - 2 + e, j)
 
     for k in ("comb", "up", "down", "thr", "corr", "gain", "shift", "cot"):
         loads[k].wait()
@@ -313,13 +320,13 @@
     cpt[...] = cp[...].T
     for i in range(6):
         x = (raw_corr, raw_gain, raw_shift)[i // 2][...].astype(F32)
-        vbuf[i * D : (i + 1) * D, :] = columns(x[i % 2 : i % 2 + 1, :])[0:D, :]
+        bias[up_to(D, 16) : up_to(D, 16) + D, i * 128 : (i + 1) * 128] = columns(x[i % 2 : i % 2 + 1, :])[0:D, :]
     one_row = jnp.where(lax.broadcasted_iota(jnp.int32, (8, T), 0) == 0, 1.0, 0.0).astype(BF)
     first_low[D : D + 8, :] = one_row
     acc[...] = jnp.zeros_like(acc)
 
     def vec(i):
-        return wide(vbuf[i * D : (i + 1) * D, :])
+        return wide(bias[up_to(D, 16) : up_to(D, 16) + D, i * 128 : (i + 1) * 128])
 
     def norm(x):
         x = x - jnp.mean(x, 0, keepdims=True)
@@ -338,38 +345,46 @@
     HC = hst // 2
 
     def send_out(b):
-        t = pl.ds(pl.multiple_of(b * BT, BT), BT)
+        t = slice(b * BT, (b + 1) * BT)
         there = pl.ds(pl.multiple_of(me * T + b * BT, BT), BT)
         return remote(cot.at[:, t], lo_out.at[:, there], osend.at[b], orecv.at[b], peer)
 
-    def middle(b, carry):
-        t = pl.ds(pl.multiple_of(b * BT, BT), BT)
+    def block_stages(b):
+        t = slice(b * BT, (b + 1) * BT)
         att = mm(cpt[...], ctx[:, t])
+        yield
         x1, rs1 = norm(tok[:, t].astype(F32) + att + vec(0))
         first = x1 * vec(2) + vec(4)
         low = first.astype(BF)
         first_low[0:D, t] = low
+        yield
         for j in range(4):
             u = slice(j * HC, (j + 1) * HC)
             pre = mm(upt[u, :], low) + wide(thr_buf[u, :])
             cdf, pdf = phi_pair(pre)
             act[u, t] = (pre * cdf).astype(BF)
             dpre[u, t] = (cdf + pre * pdf).astype(BF)
+            yield
         dn = mm(raw_down[0], act[0:hid, t]) + mm(raw_down[1], act[hst : hst + hid, t])
+        yield
         x2, rs2 = norm(first + dn + vec(1))
         dy = cot[:, t].astype(F32)
         cot[:, t] = (x2 * vec(3) + vec(5)).astype(BF)
-        send_out(b).start()
         tally(0, dy * x2)
         tally(1, dy)
         dr2 = norm_back(dy, x2, rs2, vec(3))
         tally(2, dr2)
         dd = dr2.astype(BF)
         d_down[:, t] = dd
+        if b < EARLY:
+            send_out(b).start()
+        yield
         for j in range(4):
             u = slice(j * HC, (j + 1) * HC)
             dpre[u, t] = (mm(downn[u, :], dd) * dpre[u, t].astype(F32)).astype(BF)
+            yield
         df = dr2 + mm(raw_up[0], dpre[0:hid, t]) + mm(raw_up[1], dpre[hst : hst + hid, t])
+        yield
         tally(3, df * x1)
         tally(4, df)
         dr1 = norm_back(df, x1, rs1, vec(2))
@@ -377,10 +392,16 @@
         bias[0:D, t] = dr1
         da = dr1.astype(BF)
         d_att[:, t] = da
+        yield
         dctx[:, t] = mm(cp[...], da).astype(BF)
-        return carry
-
-    lax.fori_loop(0, T // BT, middle, 0)
+        yield
+
+    blocks = T // BT
+    runs = [block_stages(b) for b in range(blocks)]
+    for k in range(STAGES + LAG * (blocks - 1)):
+        for b in range(blocks):
+            if 0 <= k - LAG * b < STAGES:
+                next(runs[b])
 
     def all_of(ref, sem):
         pltpu.make_async_copy(ref, ref, sem).wait()
@@ -520,6 +541,7 @@
                 r[f"buf{gs}"][c, s, bs + l * 16 : bs + (l + 1) * 16, 0:wl] = x
     clear(gu, plan.used[gu])
     step(gu, 1)
+    step(gd, 2)
     first_low[0:D, :] = tok[...]
 
     lo_here = pltpu.make_async_copy(cot, lo_out.at[:, mine], lsem.at[13])
@@ -534,49 +556,82 @@
 
     last = len(plan.rows) - 1
 
-    def backward_head(i, carry):
-        h = lax.rem(i, 2) * hs + lax.div(i, 2)
-        hq = pl.ds(pl.multiple_of(h * TRIPLE, PAD), PAD)
-        hk = pl.ds(pl.multiple_of(h * TRIPLE + PAD, PAD), PAD)
-        hv = pl.ds(pl.multiple_of(h * TRIPLE + 2 * PAD, PAD), PAD)
-        rowi = lax.broadcasted_iota(jnp.int32, (PAD, T), 0)
-        scaled = (dctx[pl.ds(pl.multiple_of(h * PAD, PAD), PAD), :].astype(F32) * inv[h]).astype(BF).astype(F32)
-        nd = -jnp.sum(scaled * ctx32[h], 0, keepdims=True)
-        nh = nd.astype(BF).astype(F32)
-        da = jnp.where(rowi == HEAD_DIM, nh, jnp.where(rowi == HEAD_DIM + 1, nd - nh, scaled)).astype(BF)
-        k_buf[...] = qkv[hv, :].T
-        qt, kt = qkv[hq, :], qkv[hk, :]
-        dq = jnp.zeros((PAD, T), F32)
-        for j in range(T // BT):
+    w_rows = up_to(D, 16)
+    w_end = -(-2 * srows // T) * w_rows
+    turned_p = [upt.at[0:T, 0:BT], downn.at[0:T, 0:BT]]
+    free = up_to(w_end, 16)
+
+    def turned_s(u, x=None):
+        out = []
+        for z in range(2):
+            ls = slice((2 * u + z) * BT, (2 * u + z + 1) * BT)
+            if x is not None:
+                dpre[free : free + T // 2, ls] = x[z * (T // 2) : (z + 1) * (T // 2), :]
+            else:
+                out.append(dpre[free : free + T // 2, ls])
+        return out
+
+    def backward_pair(i, carry):
+        heads_of = [i, hs + i]
+        at = [[pl.ds(pl.multiple_of(h * TRIPLE + p * PAD, PAD), PAD) for p in range(3)] for h in heads_of]
+        for e, h in enumerate(heads_of):
+            rowi = lax.broadcasted_iota(jnp.int32, (PAD, T), 0)
+            scaled = (dctx[pl.ds(pl.multiple_of(h * PAD, PAD), PAD), :].astype(F32) * inv[h]).astype(BF).astype(F32)
+            nd = -jnp.sum(scaled * ctx32[h], 0, keepdims=True)
+            nh = nd.astype(BF).astype(F32)
+            da_buf[e] = jnp.where(rowi == HEAD_DIM, nh, jnp.where(rowi == HEAD_DIM + 1, nd - nh, scaled)).astype(BF)
+            k_buf[e] = qkv[at[e][2], :].T
+        dq = [None, None]
+
+        def score_grads(u):
+            e, j = divmod(u, nq)
             rr = slice(j * BT, (j + 1) * BT)
-            pk = probs[h, rr, :]
-            dxt[hv, rr] = mm(da, pk, NT).astype(BF)
-            ds = (pk.astype(F32) * mm(k_buf[rr, :], da)).astype(BF)
-            dxt[hk, rr] = (mm(qt, ds, NT) * (1.0 / LOG2E)).astype(BF)
-            dq = dq + mm(kt[:, rr], ds)
-        dxt[hq, :] = (dq * SCALE).astype(BF)
-
-        for at, todo in plan.schedule.items():
-            @pl.when(i == at)
+            pk = probs[heads_of[e], rr, :]
+            turned_p[u % 2][...] = pk.T
+            ds = (pk.astype(F32) * mm(k_buf[e, rr, :], da_buf[e])).astype(BF)
+            turned_s(u % 2, ds.T)
+            return ds
+
+        def products(u, ds):
+            e, j = divmod(u, nq)
+            hq, hk, hv = at[e]
+            rr = slice(j * BT, (j + 1) * BT)
+            dxt[hv, rr] = mm(da_buf[e], turned_p[u % 2][...]).astype(BF)
+            x, y = turned_s(u % 2)
+            dk = mm(qkv[hq, 0 : T // 2], x) + mm(qkv[hq, T // 2 : T], y)
+            dxt[hk, rr] = (dk * (1.0 / LOG2E)).astype(BF)
+            z = mm(qkv[hk, rr], ds)
+            dq[e] = z if j == 0 else dq[e] + z
+            if j == nq - 1:
+                dxt[hq, :] = (dq[e] * SCALE).astype(BF)
+
+        held_ds = None
+        for u in range(2 * nq + 1):
+            now = score_grads(u) if u < 2 * nq else None
+            if held_ds is not None:
+                products(u - 1, held_ds)
+            held_ds = now
+
+        for when, todo in plan.schedule.items():
+            @pl.when(i == when)
             def _(todo=todo):
                 for what in todo:
-                    if what == "part0":
+                    if what == "lo":
+                        for b in range(EARLY, T // BT):
+                            send_out(b).start()
+                    elif what == "part0":
                         part_grads(0)
                     else:
                         step(*what)
         return carry
 
-    lax.fori_loop(0, heads, backward_head, 0)
+    for a in range(0, 2 * srows, T):
+        b = min(T, 2 * srows - a)
+        o = a // T * w_rows
+        dpre[o : o + D, 0:b] = wt[a : a + b, :].T
+    lax.fori_loop(0, hs, backward_pair, 0)
 
     part_grads(len(plan.parts) - 1)
-    w_rows = up_to(D, 16)
-
-    def turn_weights():
-        for a in range(0, 2 * srows, T):
-            b = min(T, 2 * srows - a)
-            o = a // T * w_rows
-            dpre[o : o + D, 0:b] = wt[a : a + b, :].T
-
     def input_block(b):
         t = slice(b * BT, (b + 1) * BT)
         x = bias[0:D, t]
@@ -594,9 +649,7 @@
     dx_here = pltpu.make_async_copy(bias.at[0:D, :], dxo_out, lsem.at[14])
     done, sent = 0, None
     for what in plan.after:
-        if what == "w":
-            turn_weights()
-        elif what == "send":
+        if what == "send":
             sent = 0
         elif isinstance(what, int):
             input_block(what)
@@ -729,7 +782,7 @@
         "wt": V((2 * R, D), BF), "cp": V((2 * W, D), BF), "cpt": V((D, 2 * W), BF), "upt": V((2 * hst, D), BF), "downn": V((2 * hst, D), BF),
         "qkv": V((2 * R, T), BF), "bias": V((T, T), F32), "probs": V((2 * hs, T, T), BF), "ctx32": V((2 * hs, PAD, T), F32), "ctx": V((2 * W, T), BF),
         "inv": V((2 * hs, 1, T), F32), "dctx": V((2 * W, T), BF), "dxt": V((max(2 * R, 2 * hst), T), BF), "dpre": V((2 * hst, T), BF),
-        "vbuf": V((6 * D, 128), F32), "thr_buf": V((2 * hst, 128), F32), "off_buf": V((2 * R, 128), F32), "acc": V((D, 128), F32), "k_buf": V((T, PAD), BF),
+        "thr_buf": V((max(2 * hst, 2 * R), 128), F32), "acc": V((D, 128), F32), "k_buf": V((2, T, PAD), BF), "da_buf": V((2, PAD, T), BF),
         "rows": V((T // 128, 128), jnp.int32), "cols": V((T // 128, 128), jnp.int32),
         "lsem": sem((15,)), "wsend": sem((6, 2)), "wrecv": sem((6,)), "gsend": sem((G, 9)), "grecv": sem((G, 9)), "gloc": sem((G,)),
         "osend": sem((T // BT,)), "orecv": sem((T // BT,)), "xsend": sem((T // BT,)), "xrecv": sem((T // BT,)),

time: 112 us -> 93.5 us (0.83)
  Pallas kernels: 109 us -> 90.1 us
    pallas_call x1, Pallas kernels: 104 us -> 85.3 us  [shards(): pl.pallas_call(functools.partial(main_kernel, n, hs, plan, list(INPUTS) +...]
where the time goes in v3:
time: 93.5 us; the launch traced here: 93.3 us
  Pallas kernels  90.1 us (96%)
  other arithmetic  1.29 us (1%)
  local copies, waits for them, and re-layouts  1.26 us (1%)
    pallas_call x1, Pallas kernels, shards(): pl.pallas_call(functools.partial(main_kernel, n, hs, plan, list(INPUTS) +...  85.3 us
    pallas_call x1, Pallas kernels, shards(): pl.pallas_call(functools.partial(final_kernel, hs, plan), out_shape=[jax....  4.82 us

profile of v3, /device:TPU:0, one launch (start us, length us, event | category | flops | bytes accessed | tf_op | source)
XLA Modules:
  0.0 93.3 jit_solution(9491533915784694169)
XLA Ops:
  0.6 1.3 %reshape.34.refs_6_ = bf16[1,600]{1,0:T(2,128)(2,1)} reshape(bf16[600]{0:T(1024)(128)(2,1)} %param.19) | data formatting | bytes 2400 | tf_op jit(solution)/shard_map/reshape | solution.py:769
  1.9 85.3 %shard_map.221 = (bf16[312,2048]{1,0:T(8,128)(2,1)}, f32[312,1024]{1,0:T(8,128)}, bf16[312,1024]{1,0:T(8,128)(2,1)}, bf16[2,832,128]{2,1,0:T(8,128)(2,1)}, bf16[...) custom-call(bf16[312,2048]{1,0:T(8,128)(2,1)} %bitcast.10, ...), custom_call_target="tpu_custom_call" | custom-call | tf_op jit(solution)/shard_map/pallas_call | solution.py:801
  87.2 4.8 %shard_map.222 = (bf16[312,2048]{1,0:T(8,128)(2,1)}, f32[312,2048]{1,0:T(8,128)}, f32[3,156,312]{2,1,0:T(8,128)}, f32[2,156]{1,0:T(2,128)}, f32[156,312]{1,0:T(8...) custom-call(bf16[312,2048]{1,0:T(8,128)(2,1)} %get-tuple-element.29., ...), custom_call_target="tpu_custom_call" | custom-call | tf_op jit(solution)/shard_map/pallas_call | solution.py:813
  92.0 1.3 %reduce = f32[600]{0:T(1024)} reduce(f32[1,600]{1,0:T(1,128)} %get-tuple-element.42, f32[]{:T(128)} %constant.1), dimensions={0}, to_apply=%get-tuple-element.42.reduce_sub_computation | reduce | bytes 4804 | tf_op jit(solution)/shard_map/pallas_call | solution.py:813

commit v4 on v3

--- a/solution.py
+++ b/solution.py
@@ -86,7 +86,7 @@
 
 
 PARTS = (4, 2)
-LAG, STAGES, EARLY = 1, 15, 2
+LAG, STAGES, EARLY = 1, 15, 3
 FLAT = (False, False, False, True)
 SCHEDULE = {0: [(1, 2)], 2: [(0, 3)], 3: ["lo", "part0", (2, 1), (0, 4), (1, 3)], 4: [(2, 2), (0, 5)], 5: [(0, 6), (1, 4)]}
 AFTER = [(3, 1), 0, (3, 2), "send", 1, (2, 3), (0, 7), (1, 5), 2, 3, (3, 3), (2, 4), (1, 6), (3, 4), (2, 5), (1, 7), (2, 6), (3, 5), (2, 7), (3, 6)]

time: 93.5 us -> 93.8 us (level)
  no operation moved by 1% of the time
where the time goes in v4:
time: 93.8 us; the launch traced here: 93.6 us
  Pallas kernels  90.3 us (96%)
  other arithmetic  1.29 us (1%)
  local copies, waits for them, and re-layouts  1.26 us (1%)
    pallas_call x1, Pallas kernels, shards(): pl.pallas_call(functools.partial(main_kernel, n, hs, plan, list(INPUTS) +...  85.5 us
    pallas_call x1, Pallas kernels, shards(): pl.pallas_call(functools.partial(final_kernel, hs, plan), out_shape=[jax....  4.82 us

profile of v4, /device:TPU:0, one launch (start us, length us, event | category | flops | bytes accessed | tf_op | source)
XLA Modules:
  0.0 93.6 jit_solution(9334165402754550205)
XLA Ops:
  0.6 1.3 %reshape.34.refs_6_ = bf16[1,600]{1,0:T(2,128)(2,1)} reshape(bf16[600]{0:T(1024)(128)(2,1)} %param.19) | data formatting | bytes 2400 | tf_op jit(solution)/shard_map/reshape | solution.py:769
  1.9 85.5 %shard_map.221 = (bf16[312,2048]{1,0:T(8,128)(2,1)}, f32[312,1024]{1,0:T(8,128)}, bf16[312,1024]{1,0:T(8,128)(2,1)}, bf16[2,832,128]{2,1,0:T(8,128)(2,1)}, bf16[...) custom-call(bf16[312,2048]{1,0:T(8,128)(2,1)} %bitcast.10, ...), custom_call_target="tpu_custom_call" | custom-call | tf_op jit(solution)/shard_map/pallas_call | solution.py:801
  87.4 4.8 %shard_map.222 = (bf16[312,2048]{1,0:T(8,128)(2,1)}, f32[312,2048]{1,0:T(8,128)}, f32[3,156,312]{2,1,0:T(8,128)}, f32[2,156]{1,0:T(2,128)}, f32[156,312]{1,0:T(8...) custom-call(bf16[312,2048]{1,0:T(8,128)(2,1)} %get-tuple-element.29., ...), custom_call_target="tpu_custom_call" | custom-call | tf_op jit(solution)/shard_map/pallas_call | solution.py:813
  92.3 1.3 %reduce = f32[600]{0:T(1024)} reduce(f32[1,600]{1,0:T(1,128)} %get-tuple-element.42, f32[]{:T(128)} %constant.1), dimensions={0}, to_apply=%get-tuple-element.42.reduce_sub_computation | reduce | bytes 4804 | tf_op jit(solution)/shard_map/pallas_call | solution.py:813
